TPU v7x, 128 devices: a whole 4x4x4 slice. The times are simulated.
128 devices in a mesh: dp: 8 (over z, x_hi), pair: 16 (over x_lo, y, core).
Axes of the slice: x: 4 (x_hi: 2, x_lo: 2; x = x_hi * 2 + x_lo), y: 4, z: 4, core: 2. Of those that a mesh axis runs over, the one named last changes fastest.
Arguments:
- pair_in: bfloat16 [1024, 128, 128], P(('dp', 'pair')), parts along dimension 0, may hold values from -170 to 170
- cotangent: bfloat16 [1024, 128, 128], P(('dp', 'pair')), parts along dimension 0, may hold values from -6 to 6
- in_gain: float32 [2, 128], replicated, may hold values from 0.1 to 1.9
- proj_weight: bfloat16 [2, 128, 512], replicated, may hold values from -0.5 to 0.5
- gate_weight: bfloat16 [2, 128, 128], replicated, may hold values from -0.5 to 0.5
- mid_gain: float32 [2, 128], replicated, may hold values from 0.1 to 1.9
- out_weight: bfloat16 [2, 128, 128], replicated, may hold values from -0.5 to 0.5
Outputs:
- pair_grad: bfloat16 [1024, 128, 128], P(('dp', 'pair')), parts along dimension 0
- proj_grad: float32 [16, 128, 512], P('dp'), parts along dimension 0
- gate_grad: float32 [16, 128, 128], P('dp'), parts along dimension 0
- out_grad: float32 [16, 128, 128], P('dp'), parts along dimension 0
- in_gain_grad: float32 [16, 128], P('dp'), parts along dimension 0
- mid_gain_grad: float32 [16, 128], P('dp'), parts along dimension 0
There are 8 independent parts, one for each index of `dp`. A program takes and returns all parts, laid end to end along the dimension named above; an argument that names none is the same for every part. Nothing has to cross between parts.
All inputs are finite; a program needn't handle non-finite values.
Results may differ from a plain program's by a relative error of at most 0.03.
Values may be sent and summed in bfloat16 or wider, within the bound.
A program may use at most 128 MiB of HBM per device.

v0:
```python
import jax
import jax.numpy as jnp
from jax import lax
from jax.sharding import PartitionSpec as P

EPSILON = 1e-05


def norm_forward(values, gain_vec):
    centre = jnp.mean(values, axis=-1, keepdims=True)
    shifted = values - centre
    inverse = lax.rsqrt(jnp.mean(shifted * shifted, axis=-1, keepdims=True) + EPSILON)
    unit_rows = shifted * inverse
    return (unit_rows * gain_vec, unit_rows, inverse)


def norm_backward(grad_rows, unit_rows, inverse, gain_vec):
    scaled = grad_rows * gain_vec
    mean_one = jnp.mean(scaled, axis=-1, keepdims=True)
    mean_two = jnp.mean(scaled * unit_rows, axis=-1, keepdims=True)
    grad_input = inverse * (scaled - mean_one - unit_rows * mean_two)
    channels = unit_rows.shape[-1]
    grad_gain = jnp.sum((grad_rows * unit_rows).reshape(-1, channels), axis=0)
    return (grad_input, grad_gain)


def cell_contract(first, second):
    flat_first = first.reshape(-1, first.shape[-1])
    flat_second = second.reshape(-1, second.shape[-1])
    return lax.dot_general(
        flat_first, flat_second, (((0,), (0,)), ((), ())), preferred_element_type=jnp.float32
    )


def project_rows(state_rows, gain_vec, proj_mat, gate_mat):
    normed, unit_rows, inverse = norm_forward(state_rows.astype(jnp.float32), gain_vec)
    normed_b = normed.astype(jnp.bfloat16)
    projected = jnp.dot(normed_b, proj_mat, preferred_element_type=jnp.float32)
    gate_pre = jnp.dot(normed_b, gate_mat, preferred_element_type=jnp.float32)
    hidden_width = proj_mat.shape[1] // 4
    left_rows = (
        jax.nn.sigmoid(projected[..., :hidden_width])
        * projected[..., hidden_width : 2 * hidden_width]
    ).astype(jnp.bfloat16)
    right_rows = (
        jax.nn.sigmoid(projected[..., 2 * hidden_width : 3 * hidden_width])
        * projected[..., 3 * hidden_width :]
    ).astype(jnp.bfloat16)
    return (unit_rows, inverse, normed_b, projected, gate_pre, left_rows, right_rows)


def finish_rows(state_rows, product, saved, gain_vec, out_mat):
    mixed, mix_unit, mix_inverse = norm_forward(product, gain_vec)
    mixed_rows = mixed.astype(jnp.bfloat16)
    output = jnp.dot(mixed_rows, out_mat, preferred_element_type=jnp.float32)
    gate_value = jax.nn.sigmoid(saved[4])
    new_state = (state_rows.astype(jnp.float32) + gate_value * output).astype(jnp.bfloat16)
    return (new_state, (mix_unit, mix_inverse, mixed_rows, output, gate_value))


def back_head(gradient, finished, gain_vec, out_mat):
    mix_unit, mix_inverse, mixed_rows, output, gate_value = finished
    gate_back = gradient * output * gate_value * (1.0 - gate_value)
    grad_output = (gradient * gate_value).astype(jnp.bfloat16)
    grad_mixed = jnp.dot(grad_output, out_mat.T, preferred_element_type=jnp.float32)
    weight_part = cell_contract(mixed_rows, grad_output)
    grad_product, gain_part = norm_backward(grad_mixed, mix_unit, mix_inverse, gain_vec)
    return (grad_product.astype(jnp.bfloat16), gate_back, weight_part, gain_part)


def back_tail(gradient, gate_back, grad_left, grad_right, saved, gain_vec, proj_mat, gate_mat):
    unit_rows, inverse, normed_b, projected, gate_pre, left_rows, right_rows = saved
    hidden_width = proj_mat.shape[1] // 4
    sigma_left = jax.nn.sigmoid(projected[..., :hidden_width])
    sigma_right = jax.nn.sigmoid(projected[..., 2 * hidden_width : 3 * hidden_width])
    value_left = projected[..., hidden_width : 2 * hidden_width]
    value_right = projected[..., 3 * hidden_width :]
    pieces = [
        grad_left * value_left * sigma_left * (1.0 - sigma_left),
        grad_left * sigma_left,
        grad_right * value_right * sigma_right * (1.0 - sigma_right),
        grad_right * sigma_right,
    ]
    grad_proj = jnp.concatenate(pieces, axis=-1).astype(jnp.bfloat16)
    gate_term = gate_back.astype(jnp.bfloat16)
    grad_normed = jnp.dot(grad_proj, proj_mat.T, preferred_element_type=jnp.float32) + jnp.dot(
        gate_term, gate_mat.T, preferred_element_type=jnp.float32
    )
    proj_part = cell_contract(normed_b, grad_proj)
    gate_part = cell_contract(normed_b, gate_term)
    grad_input, gain_part = norm_backward(grad_normed, unit_rows, inverse, gain_vec)
    return (gradient + grad_input, proj_part, gate_part, gain_part)


def on_device(pair_in, cotangent, in_gain, proj_weight, gate_weight, mid_gain, out_weight):
    columns = pair_in.shape[1]
    saved_out = project_rows(pair_in, in_gain[0], proj_weight[0], gate_weight[0])
    left_out, right_out = (saved_out[5], saved_out[6])
    product_out = jnp.einsum(
        "ikc,jkc->ijc",
        left_out,
        lax.all_gather(right_out, "pair", axis=0, tiled=True),
        preferred_element_type=jnp.float32,
    )
    state_mid, finish_out = finish_rows(pair_in, product_out, saved_out, mid_gain[0], out_weight[0])
    saved_in = project_rows(state_mid, in_gain[1], proj_weight[1], gate_weight[1])
    left_in, right_in = (saved_in[5], saved_in[6])
    left_cols = lax.all_to_all(left_in, "pair", split_axis=1, concat_axis=0, tiled=True)
    window = left_cols
    product_in = jnp.einsum(
        "kic,kjc->ijc",
        window,
        lax.all_gather(right_in, "pair", axis=0, tiled=True),
        preferred_element_type=jnp.float32,
    )
    finish_in = finish_rows(state_mid, product_in, saved_in, mid_gain[1], out_weight[1])[1]
    gradient = cotangent.astype(jnp.float32)
    grad_prod_in, gate_back_in, outw_in, midg_in = back_head(
        gradient, finish_in, mid_gain[1], out_weight[1]
    )
    left_cols_grad = jnp.einsum(
        "ijc,kjc->kic",
        grad_prod_in,
        lax.all_gather(right_in, "pair", axis=0, tiled=True),
        preferred_element_type=jnp.float32,
    )
    grad_left_in = lax.all_to_all(
        left_cols_grad.astype(jnp.bfloat16), "pair", split_axis=0, concat_axis=1, tiled=True
    ).astype(left_cols_grad.dtype)
    window = left_cols
    grad_right_in = lax.psum_scatter(
        jnp.einsum("ijc,kic->kjc", grad_prod_in, window, preferred_element_type=jnp.float32).astype(
            jnp.bfloat16
        ),
        "pair",
        scatter_dimension=0,
        tiled=True,
    ).astype(jnp.float32)
    gradient, projg_in, gateg_in, ing_in = back_tail(
        gradient,
        gate_back_in,
        grad_left_in,
        grad_right_in,
        saved_in,
        in_gain[1],
        proj_weight[1],
        gate_weight[1],
    )
    grad_prod_out, gate_back_out, outw_out, midg_out = back_head(
        gradient, finish_out, mid_gain[0], out_weight[0]
    )
    window = grad_prod_out
    grad_left_out = jnp.einsum(
        "ijc,jkc->ikc",
        window,
        lax.all_gather(right_out, "pair", axis=0, tiled=True),
        preferred_element_type=jnp.float32,
    )
    window = grad_prod_out
    grad_right_out = lax.psum_scatter(
        jnp.einsum("ijc,ikc->jkc", window, left_out, preferred_element_type=jnp.float32).astype(
            jnp.bfloat16
        ),
        "pair",
        scatter_dimension=0,
        tiled=True,
    ).astype(jnp.float32)
    gradient, projg_out, gateg_out, ing_out = back_tail(
        gradient,
        gate_back_out,
        grad_left_out,
        grad_right_out,
        saved_out,
        in_gain[0],
        proj_weight[0],
        gate_weight[0],
    )
    summed = (
        lax.psum(jnp.stack([projg_out, projg_in]).astype(jnp.bfloat16), "pair").astype(jnp.float32),
        lax.psum(jnp.stack([gateg_out, gateg_in]).astype(jnp.bfloat16), "pair").astype(jnp.float32),
        lax.psum(jnp.stack([outw_out, outw_in]).astype(jnp.bfloat16), "pair").astype(jnp.float32),
        lax.psum(jnp.stack([ing_out, ing_in]).astype(jnp.bfloat16), "pair").astype(jnp.float32),
        lax.psum(jnp.stack([midg_out, midg_in]).astype(jnp.bfloat16), "pair").astype(jnp.float32),
    )
    scale = 1.0 / columns
    return (
        gradient.astype(jnp.bfloat16),
        summed[0] * scale,
        summed[1] * scale,
        summed[2] * scale,
        summed[3] * scale,
        summed[4] * scale,
    )


def solution(mesh):
    return jax.shard_map(
        on_device,
        mesh=mesh,
        in_specs=(
            P(("dp", "pair"), None, None),
            P(("dp", "pair"), None, None),
            P(),
            P(),
            P(),
            P(),
            P(),
        ),
        out_specs=(
            P(("dp", "pair"), None, None),
            P("dp", None, None),
            P("dp", None, None),
            P("dp", None, None),
            P("dp", None),
            P("dp", None),
        ),
        check_vma=False,
    )
```

profile of v0, /device:TPU:1, one launch (start us, length us, event | category | flops | bytes accessed | tf_op | source)
XLA Modules:
  0.0 441.8 jit_solution(10945749760227270161)
XLA Ops:
  7.2 0.8 slice_bitcast_fusion.1
  8.0 1.1 copy.186
  9.3 1.4 fusion.89
  11.0 0.9 copy.192
  11.9 41.0 %all-gather.3.cloned.1.call-done = bf16[128,128,128]{2,1,0:T(8,128)(2,1)} async-done(((bf16[8,128,128]{2,1,0:T(8,128)(2,1)}), bf16[128,128,128]{2,1,0:T(8,128)(2,1)}) %all-gather.3.cloned.1.call-update) | async-done | bytes 4194320 | tf_op jit(solution)/shard_map/all_gather | solution.py:102
  53.0 6.7 %copy.195 = bf16[128,128,128]{1,0,2:T(8,128)(2,1)} copy(bf16[128,128,128]{2,1,0:T(8,128)(2,1)} %all-gather.3.cloned.1.call-done) | data formatting | bytes 8388608 | tf_op jit(solution)/shard_map/all_gather | solution.py:102
  59.7 4.5 %fusion.130 = (f32[8,128]{1,0:T(8,128)S(1)}, f32[8,128,128]{1,0,2:T(8,128)S(1)}) fusion(bf16[128,128,128]{1,0,2:T(8,128)(2,1)} %copy.195, bf16[8,128,128]{1,2,0:T(8,128)(2,1)S(1)} %get-tuple-element.63), kind=kOutput, calls=%fused_computation.214 | convolution fusion | flops 33684480 | bytes 4984832 | tf_op jit(solution)/shard_map/ikc,jkc->ijc/dot_general | solution.py:99
  65.0 1.2 convert_reduce_fusion.1
  66.9 1.3 copy-done.1
  68.2 1.1 multiply_convert_fusion.7
  69.3 1.8 copy.202
  71.1 1.1 copy.185
  72.3 1.9 copy.205
  74.1 4.3 all-to-all-start
  78.6 1.1 fusion.6
  79.8 0.8 copy-done.3
  80.5 1.1 fusion.102
  81.6 5.1 %all-to-all-done = bf16[8,128,128]{2,0,1:T(8,128)(2,1)} async-done(((bf16[8,128,128]{2,0,1:T(8,128)(2,1)}), bf16[8,128,128]{2,0,1:T(8,128)(2,1)}, u32[]{:S(2)}, u32[]{:S(2)}) %all-to-all-start) | async-done | bytes 262176 | tf_op jit(solution)/shard_map/all_to_all | solution.py:108
  86.7 1.7 copy.207
  88.4 1.9 copy.209
  90.4 20.0 %all-gather.5.cloned.1.call-done = bf16[128,128,128]{2,1,0:T(8,128)(2,1)} async-done(((bf16[8,128,128]{2,1,0:T(8,128)(2,1)}), bf16[128,128,128]{2,1,0:T(8,128)(2,1)}) %all-gather.5.cloned.1.call-update) | async-done | bytes 4194320 | tf_op jit(solution)/shard_map/all_gather | solution.py:124
  110.4 6.6 %copy.214 = bf16[128,128,128]{1,0,2:T(8,128)(2,1)} copy(bf16[128,128,128]{2,1,0:T(8,128)(2,1)} %all-gather.5.cloned.1.call-done) | data formatting | bytes 8388608 | tf_op jit(solution)/shard_map/all_gather | solution.py:124
  117.0 3.5 fusion.131
  120.6 1.2 multiply_reduce_fusion
  121.8 1.1 multiply_convert_fusion.6
  122.9 0.7 copy-done.11
  123.6 1.3 fusion.132
  124.9 4.7 %copy.309 = bf16[128,128,128]{2,0,1:T(8,128)(2,1)} copy(bf16[128,128,128]{2,1,0:T(8,128)(2,1)S(1)} %fusion.132) | data formatting | bytes 8388608 | tf_op jit(solution)/shard_map/ijc,kic->kjc/dot_general | solution.py:132
  129.6 5.2 %fusion.10 = bf16[128,8,128]{0,1,2:T(8,128)(2,1)} fusion(bf16[128,128,128]{1,0,2:T(8,128)(2,1)} %copy.214, bf16[8,128,128]{1,0,2:T(8,128)(2,1)} %copy-done.11), kind=kOutput, calls=%fused_computation.20 | convolution fusion | flops 33685504 | bytes 4718592 | tf_op jit(solution)/shard_map/ijc,kjc->kic/dot_general | solution.py:121
  134.8 1.9 copy.215
  136.7 4.3 all-to-all-start.1
  141.2 1.4 fusion.9
  142.7 0.7 copy-done.18
  143.4 1.8 fusion.104
  145.2 3.1 all-to-all-done.1
  148.3 1.8 copy_bitcast_fusion
  150.1 2.1 copy.217
  152.2 41.3 %reduce-scatter.3.cloned.1.call-done = bf16[8,128,128]{1,2,0:T(8,128)(2,1)} async-done(((bf16[128,128,128]{1,2,0:T(8,128)(2,1)}), bf16[8,128,128]{1,2,0:T(8,128)(2,1)}) %reduce-scatter.3.cloned.1.call-update) | async-done | bytes 262160 | tf_op jit(solution)/shard_map/reduce_scatter | solution.py:131
  193.6 2.3 multiply_convert_fusion.5
  196.0 1.0 fusion.47
  197.5 1.1 multiply_convert_fusion.2
  198.8 1.2 multiply_reduce_fusion.1
  200.4 0.7 copy-done.7
  201.1 3.3 fusion.82
  204.3 6.8 %copy.231 = bf16[128,128,128]{1,0,2:T(8,128)(2,1)} copy(bf16[128,128,128]{2,1,0:T(8,128)(2,1)} %fusion.82) | data formatting | bytes 8388608 | tf_op jit(solution)/shard_map/ijc,ikc->jkc/dot_general | solution.py:161
  211.3 1.3 fusion.21
  212.6 1.2 fusion.19
  214.3 1.3 fusion.20
  215.6 0.6 pad_maximum_fusion.8
  216.5 0.6 pad_maximum_fusion.7
  217.7 1.0 fusion.98
  218.7 0.8 copy-done
  219.6 1.2 fusion.133
  220.8 56.0 %reduce-scatter.5.cloned.1.call-done = bf16[8,128,128]{1,2,0:T(8,128)(2,1)} async-done(((bf16[128,128,128]{1,2,0:T(8,128)(2,1)}), bf16[8,128,128]{1,2,0:T(8,128)(2,1)}) %reduce-scatter.5.cloned.1.call-update) | async-done | bytes 262160 | tf_op jit(solution)/shard_map/reduce_scatter | solution.py:160
  276.8 1.4 fusion.73
  280.8 0.9 copy.245
  281.6 0.7 pad_maximum_fusion.2
  282.4 31.1 %all-reduce = (bf16[2,128]{1,0:T(2,128)(2,1)S(1)}, bf16[2,128]{1,0:T(2,128)(2,1)S(1)}) all-reduce(bf16[2,128]{1,0:T(2,128)(2,1)S(1)} %pad_maximum_fusion.9, bf16[2,128]{1,0:T(2,128)(2,1)S(1)} %copy-done.47), channel_id=1, replica_groups=mesh['dp'=8,'pair'=16] {'pair'}, use_global_device_ids=true, to_apply=%region_23.0 | all-reduce | flops 512 | bytes 2048 | tf_op jit(solution)/shard_map/psum | solution.py:182
  313.5 0.6 convert_multiply_fusion.9
  314.0 0.6 convert_multiply_fusion.8
  314.6 115.9 %all-reduce.4.cloned.1.call-done = (bf16[2,128,512]{2,1,0:T(8,128)(2,1)}, bf16[2,128,128]{2,1,0:T(8,128)(2,1)}, bf16[2,128,128]{2,1,0:T(8,128)(2,1)}) async-done(((bf16[2,128,512]{2,1,0:T(8,128)(2,1)}, bf16[2,128,128]{2,1,0:T(8,128)(2,1)}, bf16[2,128,128]{2,1,0:T(8,128)(2,1)}), (bf16[2,128,512]{2,1,0:T(8,128)(2,1)}, bf16[2,128,128]{2,1,0:T(8,128)(2,1)}, ...) | async-done | bytes 393232 | tf_op jit(solution)/shard_map/psum | solution.py:179
  430.5 1.5 convert_multiply_fusion.7
  432.0 1.5 convert_multiply_fusion.6
  433.5 1.8 convert_multiply_fusion.5
  (134 shorter events, 7.7 us)
Async XLA Ops:
  7.2 45.8 %all-gather.3.cloned.1.call-start = ((), (), s32[]{:S(2)}) async-start(), calls=%async_computation.4 | async-start | bytes 4456448 | tf_op jit(solution)/shard_map/all_gather | solution.py:102
  8.0 203.2 %copy-start.40 = (f32[128]{0:T(128)}, f32[128]{0:T(128)S(1)}, u32[]{:S(2)}) copy-start(f32[128]{0:T(128)S(1)} %get-tuple-element.71) | copy-start | bytes 1540
  8.0 208.3 %copy-start.43 = (f32[128]{0:T(128)}, f32[128]{0:T(128)S(1)}, u32[]{:S(2)}) copy-start(f32[128]{0:T(128)S(1)} %get-tuple-element.72) | copy-start | bytes 1540
  10.7 1.2 copy-start.45
  11.0 48.7 %copy-start.5 = (bf16[8,128,128]{1,2,0:T(8,128)(2,1)}, bf16[8,128,128]{1,2,0:T(8,128)(2,1)S(1)}, u32[]{:S(2)}) copy-start(bf16[8,128,128]{1,2,0:T(8,128)(2,1)S(1)} %get-tuple-element.63) | copy-start | bytes 786436
  11.9 98.5 %all-gather.5.cloned.1.call-start = ((), (), s32[]{:S(2)}) async-start(), calls=%async_computation.5 | async-start | bytes 4456448 | tf_op jit(solution)/shard_map/all_gather | solution.py:124
  59.7 4.9 %copy-start.33 = (bf16[2,128,128]{2,1,0:T(8,128)(2,1)S(1)}, bf16[2,128,128]{2,1,0:T(8,128)(2,1)}, u32[]{:S(2)}) copy-start(bf16[2,128,128]{2,1,0:T(8,128)(2,1)} %param.13) | copy-start | bytes 196612
  64.2 0.9 copy-start.34
  64.6 2.3 copy-start.12
  64.6 1.8 copy-start.22
  65.0 1.3 copy-start.13
  66.9 1.3 copy-start.1
  74.1 12.6 %all-to-all-start = ((bf16[8,128,128]{2,0,1:T(8,128)(2,1)}), bf16[8,128,128]{2,0,1:T(8,128)(2,1)}, u32[]{:S(2)}, u32[]{:S(2)}) async-start(bf16[8,128,128]{2,0,1:T(8,128)(2,1)} %copy.205), calls=%async_computation | async-start | bytes 524288 | tf_op jit(solution)/shard_map/all_to_all | solution.py:108
  78.4 115.2 %reduce-scatter.3.cloned.1.call-start = ((), (), s32[]{:S(2)}) async-start(), calls=%async_computation.6 | async-start | bytes 4456448 | tf_op jit(solution)/shard_map/reduce_scatter | solution.py:131
  79.7 0.8 copy-start.3
  117.0 3.6 copy-start.2
  120.4 3.2 copy-start.10
  122.9 0.7 copy-start.11
  136.7 11.7 %all-to-all-start.1 = ((bf16[128,8,128]{2,1,0:T(8,128)(2,1)}), bf16[128,8,128]{2,1,0:T(8,128)(2,1)}, u32[]{:S(2)}, u32[]{:S(2)}) async-start(bf16[128,8,128]{2,1,0:T(8,128)(2,1)} %copy.215), calls=%async_computation.1 | async-start | bytes 524288 | tf_op jit(solution)/shard_map/all_to_all | solution.py:127
  141.0 135.8 %reduce-scatter.5.cloned.1.call-start = ((), (), s32[]{:S(2)}) async-start(), calls=%async_computation.7 | async-start | bytes 4456448 | tf_op jit(solution)/shard_map/reduce_scatter | solution.py:160
  142.7 0.7 copy-start.18
  193.5 2.4 copy-start.19
  193.5 2.4 copy-start.23
  195.9 1.1 copy-start.25
  195.9 1.1 copy-start.27
  195.9 1.1 copy-start.29
  195.9 1.0 copy-start.31
  195.9 1.4 copy-start.14
  196.0 1.5 copy-start.21
  197.0 3.0 copy-start.15
  197.0 3.0 copy-start.36
  197.0 2.9 copy-start.38
  198.5 1.4 copy-start.9
  198.5 2.5 copy-start.6
  200.3 0.7 copy-start.7
  211.1 1.5 copy-start.4
  211.1 219.4 %all-reduce.4.cloned.1.call-start = ((), (), s32[]{:S(2)}) async-start(), calls=%async_computation.8 | async-start | bytes 786432 | tf_op jit(solution)/shard_map/psum | solution.py:179
  211.2 5.0 %copy-start.17 = (bf16[8,128,128]{1,2,0:T(8,128)(2,1)S(1)}, bf16[8,128,128]{1,2,0:T(8,128)(2,1)}, u32[]{:S(2)}) copy-start(bf16[8,128,128]{1,2,0:T(8,128)(2,1)} %get-tuple-element.66) | copy-start | bytes 786436
  211.2 5.9 %copy-start.26 = (bf16[8,128,128]{1,2,0:T(8,128)(2,1)S(1)}, bf16[8,128,128]{1,2,0:T(8,128)(2,1)}, u32[]{:S(2)}) copy-start(bf16[8,128,128]{1,2,0:T(8,128)(2,1)} %copy-done.25) | copy-start | bytes 786436
  211.2 5.9 %copy-start.28 = (bf16[8,128,128]{1,2,0:T(8,128)(2,1)S(1)}, bf16[8,128,128]{1,2,0:T(8,128)(2,1)}, u32[]{:S(2)}) copy-start(bf16[8,128,128]{1,2,0:T(8,128)(2,1)} %copy-done.27) | copy-start | bytes 786436
  211.2 5.9 %copy-start.30 = (bf16[8,128,128]{1,2,0:T(8,128)(2,1)S(1)}, bf16[8,128,128]{1,2,0:T(8,128)(2,1)}, u32[]{:S(2)}) copy-start(bf16[8,128,128]{1,2,0:T(8,128)(2,1)} %copy-done.29) | copy-start | bytes 786436
  211.2 5.9 %copy-start.32 = (bf16[8,128,128]{1,2,0:T(8,128)(2,1)S(1)}, bf16[8,128,128]{1,2,0:T(8,128)(2,1)}, u32[]{:S(2)}) copy-start(bf16[8,128,128]{1,2,0:T(8,128)(2,1)} %copy-done.31) | copy-start | bytes 786436
  212.6 4.6 %copy-start.41 = (f32[128]{0:T(128)S(1)}, f32[128]{0:T(128)}, u32[]{:S(2)}) copy-start(f32[128]{0:T(128)} %copy-done.40) | copy-start | bytes 1540
  216.2 1.5 copy-start.35
  217.2 2.4 copy-start
  217.2 2.4 copy-start.8
  276.8 1.5 copy-start.44
  278.2 1.0 copy-start.20
  278.2 1.1 copy-start.24
  279.3 1.0 copy-start.16
  279.3 1.0 copy-start.37
  279.3 1.0 copy-start.39
  279.3 1.0 copy-start.42
  279.8 2.6 copy-start.46
  279.8 2.6 copy-start.47
Sparse Core Ops, SparseCore 0:
  12.0 40.9 all-gather.2
  71.3 39.0 all-gather.4
  129.7 63.7 reduce-scatter.2
  211.3 65.4 reduce-scatter.4
  313.6 116.8 all-reduce.3
where the time goes:
time: 443 us; the launch traced here: 442 us
  waiting for transfers between devices  283 us (64%)
  local copies, waits for them, and re-layouts  47.7 us (11%)
  matrix products  35.4 us (8%)
  blocking collectives  31.1 us (7%)
  other arithmetic  21.5 us (5%)
  between operations  14.4 us (3%)
  starting transfers between devices  9.16 us (2%)
    psum x1, waiting for transfers between devices, on_device(): lax.psum(jnp.stack([projg_out, projg_in]).astype(jnp.bfloat16), 'pair')  116 us
    reduce_scatter x1, waiting for transfers between devices, on_device(): lax.psum_scatter(jnp.einsum('ijc,ikc->jkc', window, left_out, preferred_e...  56 us
    reduce_scatter x1, waiting for transfers between devices, on_device(): lax.psum_scatter(jnp.einsum('ijc,kic->kjc', grad_prod_in, window, preferr...  41.3 us
    all_gather x1, waiting for transfers between devices, on_device(): lax.all_gather(right_out, 'pair', axis=0, tiled=True)  41 us
    psum x1, blocking collectives, on_device(): lax.psum(jnp.stack([ing_out, ing_in]).astype(jnp.bfloat16), 'pair')  31.1 us
    all_gather x1, waiting for transfers between devices, on_device(): lax.all_gather(right_in, 'pair', axis=0, tiled=True)  20 us
    unnamed x99, local copies, waits for them, and re-layouts  10.1 us
  transfers between devices with their start and end apart: 7, of which 7 were waited for; matrix products, arithmetic and copies ran while one was open for 7% of the time, Pallas kernels for 0%

commit v1 on v0

v1 whole, which is shorter than its diff:
```python
import functools

import jax
import jax.numpy as jnp
from jax import lax
from jax.experimental import pallas as pl
from jax.experimental.pallas import tpu as pltpu
from jax.sharding import PartitionSpec as P

EPSILON = 1e-05
MESH = pl.DeviceIdType.MESH
F32 = jnp.float32
BF16 = jnp.bfloat16

N = 128
PEERS = 16
ROWS = N // PEERS
CELLS = ROWS * N
WIDE = 2 * N
STEPS = CELLS // WIDE

TO_CH_0, TO_ROW_0, TO_CH_1, TO_ROW_1, GRAD_CH_1, GRAD_ROW_1, GRAD_CH_0, GRAD_ROW_0 = range(8)
SUM_EARLY, ALL_EARLY, SUM_LATE, ALL_LATE, GAINS = range(8, 13)
PHASES = 13


def dot(first, second, dims):
    return lax.dot_general(first, second, (dims, ((), ())), preferred_element_type=F32)


def nn(first, second):
    return dot(first, second, ((1,), (0,)))


def nt(first, second):
    return dot(first, second, ((1,), (1,)))


def tn(first, second):
    return dot(first, second, ((0,), (0,)))


def mean_channels(values):
    return jnp.sum(values, axis=0, keepdims=True) * (1.0 / N)


def norm_forward(values):
    shifted = values - mean_channels(values)
    inverse = lax.rsqrt(mean_channels(shifted * shifted) + EPSILON)
    return shifted * inverse, inverse


def norm_backward(scaled, unit, inverse):
    return inverse * (scaled - mean_channels(scaled) - unit * mean_channels(scaled * unit))


def kernel(
    pair_in, cotangent, in_gain, proj_weight, gate_weight, mid_gain, out_weight,
    pair_grad, proj_grad, gate_grad, out_grad, in_gain_grad, mid_gain_grad,
    gains, weight, weight_t, out_t,
    state0, state1, cot, grad1,
    unit, inverse, normed, sig_l, val_l, sig_r, val_r, gate, output, mix_unit, mix_inverse, mixed,
    go, gp, in_acc, mid_acc,
    turn_a, turn_b, chan_l, chan_r,
    send2, recv2, send1, recv1,
    sum_early_send, sum_early_recv, all_early, sum_late_send, sum_late_recv, all_late, gains_all,
    send_sem, recv_sem,
):
    me = lax.axis_index("pair")
    my_x, my_y, my_core = me // 8, (me // 2) % 4, me % 2

    def peer(o):
        x = (my_x + o // 8) % 2
        y = (my_y + (o // 2) % 4) % 4
        core = (my_core + o % 2) % 2
        return x * 8 + y * 2 + core

    def copy_to(phase, src, dst, target):
        return pltpu.make_async_remote_copy(
            src_ref=src, dst_ref=dst,
            send_sem=send_sem.at[phase, target], recv_sem=recv_sem.at[phase, me],
            device_id={"pair": target}, device_id_type=MESH,
        )

    def send_all(phase, src_of, dst):
        @pl.loop(0, PEERS - 1)
        def _(i):
            target = peer(PEERS - 1 - i)
            copy_to(phase, src_of(target), dst, target).start()

    def wait_all(phase, slot_of):
        @pl.loop(1, PEERS)
        def _(o):
            source = peer(o)
            pltpu.make_async_copy(slot_of(source), slot_of(source), recv_sem.at[phase, source]).wait()

    def wait_sent(phase, src_of):
        @pl.loop(1, PEERS)
        def _(o):
            target = peer(o)
            pltpu.make_async_copy(src_of(target), src_of(target), send_sem.at[phase, target]).wait()

    barrier = pltpu.get_barrier_semaphore()

    @pl.loop(1, PEERS)
    def _(o):
        pl.semaphore_signal(barrier, inc=1, device_id={"pair": peer(o)}, device_id_type=MESH)

    for l in range(2):
        for table, source in ((0, in_gain), (1, mid_gain)):
            row = jnp.broadcast_to(source[l : l + 1, :], (N, N)).T
            gains[2 * l + table] = jnp.concatenate([row, row], axis=1)
        for f in range(4):
            block = proj_weight[l, :, f * N : (f + 1) * N]
            weight[l, :, f * N : (f + 1) * N] = block
            weight_t[l, f * N : (f + 1) * N, :] = block.astype(F32).T.astype(BF16)
        weight[l, :, 4 * N :] = gate_weight[l]
        weight_t[l, 4 * N :, :] = gate_weight[l].astype(F32).T.astype(BF16)
        out_t[l] = out_weight[l].astype(F32).T.astype(BF16)

    for a in range(ROWS):
        state0[:, a * N : (a + 1) * N] = pair_in[a].astype(F32).T

    in_acc[...] = jnp.zeros_like(in_acc)
    mid_acc[...] = jnp.zeros_like(mid_acc)

    def lanes(p):
        return pl.ds(pl.multiple_of(p * WIDE, WIDE), WIDE)

    def put_turned(ref, p, values):
        for h in range(2):
            ref[pl.ds(2 * p + h, N, stride=ROWS), :] = values[:, h * N : (h + 1) * N]

    def get_turned(ref, p):
        return jnp.concatenate([ref[pl.ds(2 * p + h, N, stride=ROWS), :] for h in range(2)], axis=1)

    def project(l, p, state):
        at = lanes(p)
        unit_p, inverse_p = norm_forward(state)
        normed_p = (unit_p * gains[2 * l]).astype(BF16)
        unit[l, :, at] = unit_p
        inverse[l, :, at] = inverse_p
        normed[l, :, at] = normed_p
        projected = nn(weight_t[l], normed_p)
        sig = jax.nn.sigmoid(projected[0:N])
        val = projected[N : 2 * N]
        sig_l[l, :, at] = sig
        val_l[l, :, at] = val
        put_turned(turn_a, p, sig * val)
        sig = jax.nn.sigmoid(projected[2 * N : 3 * N])
        val = projected[3 * N : 4 * N]
        sig_r[l, :, at] = sig
        val_r[l, :, at] = val
        put_turned(turn_b, p, sig * val)
        gate[l, :, at] = jax.nn.sigmoid(projected[4 * N :])

    def send_two(slot, phase):
        @pl.loop(0, PEERS)
        def _(d):
            rows = pl.ds(pl.multiple_of(d * ROWS * ROWS, ROWS * ROWS), ROWS * ROWS)
            send2[slot, d, 0:64, :] = turn_a[rows, :].astype(BF16)
            send2[slot, d, 64:128, :] = turn_b[rows, :].astype(BF16)

        send_all(phase, lambda d: send2.at[slot, d], recv2.at[slot, me])
        recv2[slot, me] = send2[slot, me]

    def send_one(slot, phase):
        @pl.loop(0, PEERS)
        def _(d):
            rows = pl.ds(pl.multiple_of(d * ROWS * ROWS, ROWS * ROWS), ROWS * ROWS)
            send1[slot, d] = turn_a[rows, :].astype(BF16)

        send_all(phase, lambda d: send1.at[slot, d], recv1.at[slot, me])
        recv1[slot, me] = send1[slot, me]

    def take_two(slot, phase):
        wait_all(phase, lambda s: recv2.at[slot, s])

        @pl.loop(0, PEERS)
        def _(s):
            rows = pl.ds(pl.multiple_of(s * ROWS * ROWS, ROWS * ROWS), ROWS * ROWS)
            turn_a[rows, :] = recv2[slot, s, 0:64, :].astype(F32)
            turn_b[rows, :] = recv2[slot, s, 64:128, :].astype(F32)

    def take_one(slot, phase):
        wait_all(phase, lambda s: recv1.at[slot, s])

        @pl.loop(0, PEERS)
        def _(s):
            rows = pl.ds(pl.multiple_of(s * ROWS * ROWS, ROWS * ROWS), ROWS * ROWS)
            turn_a[rows, :] = recv1[slot, s].astype(F32)

    def two_channels(block):
        wide = block.astype(F32).reshape(PEERS, 2, ROWS, N)
        return [wide[:, h].reshape(N, N).astype(BF16) for h in range(2)]

    def join_channels(first, second):
        pair = jnp.stack([first.reshape(PEERS, ROWS, N), second.reshape(PEERS, ROWS, N)], axis=1)
        return pair.reshape(PEERS, 2 * ROWS, N).astype(BF16)

    def channel_forward(l, slot2, slot1, phase_in, phase_out):
        wait_all(phase_in, lambda s: recv2.at[slot2, s])
        for q in range(ROWS // 2):
            lefts = two_channels(recv2[slot2, :, 16 * q : 16 * q + 16, :])
            rights = two_channels(recv2[slot2, :, 64 + 16 * q : 64 + 16 * q + 16, :])
            products = []
            for h in range(2):
                chan_l[l, 2 * q + h] = lefts[h]
                chan_r[l, 2 * q + h] = rights[h]
                products.append(nt(lefts[h], rights[h]) if l == 0 else tn(lefts[h], rights[h]))
            send1[slot1, :, 16 * q : 16 * q + 16, :] = join_channels(*products)
        send_all(phase_out, lambda d: send1.at[slot1, d], recv1.at[slot1, me])
        recv1[slot1, me] = send1[slot1, me]

    def channel_backward(l, slot1, slot2, phase_in, phase_out):
        wait_all(phase_in, lambda s: recv1.at[slot1, s])
        for q in range(ROWS // 2):
            grads = two_channels(recv1[slot1, :, 16 * q : 16 * q + 16, :])
            lefts, rights = [], []
            for h in range(2):
                left, right = chan_l[l, 2 * q + h], chan_r[l, 2 * q + h]
                if l == 0:
                    lefts.append(nn(grads[h], right))
                    rights.append(tn(grads[h], left))
                else:
                    lefts.append(nt(right, grads[h]))
                    rights.append(nn(left, grads[h]))
            send2[slot2, :, 16 * q : 16 * q + 16, :] = join_channels(*lefts)
            send2[slot2, :, 64 + 16 * q : 64 + 16 * q + 16, :] = join_channels(*rights)
        send_all(phase_out, lambda d: send2.at[slot2, d], recv2.at[slot2, me])
        recv2[slot2, me] = send2[slot2, me]

    def finish(l, p):
        at = lanes(p)
        mix_unit_p, mix_inverse_p = norm_forward(get_turned(turn_a, p))
        mixed_p = (mix_unit_p * gains[2 * l + 1]).astype(BF16)
        mix_unit[l, :, at] = mix_unit_p
        mix_inverse[l, :, at] = mix_inverse_p
        mixed[l, :, at] = mixed_p
        output_p = nn(out_t[l], mixed_p)
        output[l, :, at] = output_p
        return output_p

    def fold(values):
        return values[:, :N] + values[:, N:]

    def back_head(l, p, gradient):
        at = lanes(p)
        gate_p = gate[l, :, at]
        go_p = (gradient * gate_p).astype(BF16)
        go[l, :, at] = go_p
        gp[l, 4 * N :, at] = (gradient * output[l, :, at] * gate_p * (1.0 - gate_p)).astype(BF16)
        grad_mixed = nn(out_weight[l], go_p)
        mix_unit_p = mix_unit[l, :, at]
        mid_acc[l] += fold(grad_mixed * mix_unit_p)
        grad_product = norm_backward(grad_mixed * gains[2 * l + 1], mix_unit_p, mix_inverse[l, :, at])
        put_turned(turn_a, p, grad_product)

    def back_tail(l, p, gradient):
        at = lanes(p)
        grad_left = get_turned(turn_a, p)
        grad_right = get_turned(turn_b, p)
        sig = sig_l[l, :, at]
        plain = grad_left * sig
        gp[l, 0:N, at] = (plain * val_l[l, :, at] * (1.0 - sig)).astype(BF16)
        gp[l, N : 2 * N, at] = plain.astype(BF16)
        sig = sig_r[l, :, at]
        plain = grad_right * sig
        gp[l, 2 * N : 3 * N, at] = (plain * val_r[l, :, at] * (1.0 - sig)).astype(BF16)
        gp[l, 3 * N : 4 * N, at] = plain.astype(BF16)
        grad_normed = nn(weight[l], gp[l, :, at])
        unit_p = unit[l, :, at]
        in_acc[l] += fold(grad_normed * unit_p)
        return gradient + norm_backward(grad_normed * gains[2 * l], unit_p, inverse[l, :, at])

    @pl.loop(0, STEPS)
    def _(p):
        project(0, p, state0[:, lanes(p)])

    pl.semaphore_wait(barrier, PEERS - 1)
    send_two(0, TO_CH_0)
    for a in range(ROWS):
        cot[:, a * N : (a + 1) * N] = cotangent[a].astype(F32).T
    channel_forward(0, 0, 0, TO_CH_0, TO_ROW_0)
    take_one(0, TO_ROW_0)

    @pl.loop(0, STEPS)
    def _(p):
        at = lanes(p)
        output_p = finish(0, p)
        state = (state0[:, at] + gate[0, :, at] * output_p).astype(BF16).astype(F32)
        state1[:, at] = state
        project(1, p, state)

    send_two(1, TO_CH_1)
    channel_forward(1, 1, 1, TO_CH_1, TO_ROW_1)
    take_one(1, TO_ROW_1)

    @pl.loop(0, STEPS)
    def _(p):
        finish(1, p)
        back_head(1, p, cot[:, lanes(p)])

    send_one(2, GRAD_CH_1)
    channel_backward(1, 2, 2, GRAD_CH_1, GRAD_ROW_1)
    take_two(2, GRAD_ROW_1)

    @pl.loop(0, STEPS)
    def _(p):
        at = lanes(p)
        gradient = back_tail(1, p, cot[:, at])
        grad1[:, at] = gradient
        back_head(0, p, gradient)

    send_one(3, GRAD_CH_0)

    def put_early(first, values):
        for i in range(N // 64):
            sum_early_send[first + i] = values[64 * i : 64 * i + 64, :].astype(BF16)

    for f in range(5):
        put_early(2 * f, nt(normed[1], gp[1, f * N : (f + 1) * N, :]))
    put_early(10, nt(mixed[1], go[1]))
    put_early(12, nt(normed[0], gp[0, 4 * N :, :]))
    put_early(14, nt(mixed[0], go[0]))
    send_all(SUM_EARLY, lambda d: sum_early_send.at[d], sum_early_recv.at[me])
    sum_early_recv[me] = sum_early_send[me]

    channel_backward(0, 3, 3, GRAD_CH_0, GRAD_ROW_0)

    wait_all(SUM_EARLY, lambda s: sum_early_recv.at[s])
    all_early[me] = jnp.sum(sum_early_recv[...].astype(F32), axis=0).astype(BF16)
    send_all(ALL_EARLY, lambda d: all_early.at[me], all_early.at[me])

    take_two(3, GRAD_ROW_0)

    @pl.loop(0, STEPS)
    def _(p):
        at = lanes(p)
        gradient = back_tail(0, p, grad1[:, at])
        for h in range(2):
            pair_grad[2 * p + h] = gradient[:, h * N : (h + 1) * N].T.astype(BF16)

    for f in range(4):
        values = nt(normed[0], gp[0, f * N : (f + 1) * N, :])
        for i in range(4):
            sum_late_send[4 * f + i] = values[32 * i : 32 * i + 32, :].astype(BF16)
    send_all(SUM_LATE, lambda d: sum_late_send.at[d], sum_late_recv.at[me])
    sum_late_recv[me] = sum_late_send[me]

    gain_rows = [jnp.sum(ref[l].T, axis=0, keepdims=True) for ref in (in_acc, mid_acc) for l in range(2)]
    gains_all[me] = jnp.concatenate(gain_rows + [jnp.zeros((4, N), F32)], axis=0)
    send_all(GAINS, lambda d: gains_all.at[me], gains_all.at[me])

    wait_all(SUM_LATE, lambda s: sum_late_recv.at[s])
    all_late[me] = jnp.sum(sum_late_recv[...].astype(F32), axis=0).astype(BF16)
    send_all(ALL_LATE, lambda d: all_late.at[me], all_late.at[me])

    scale = 1.0 / N
    wait_all(ALL_EARLY, lambda s: all_early.at[s])

    def early(first):
        return all_early[first : first + 2].astype(F32).reshape(N, N) * scale

    for f in range(4):
        proj_grad[1, :, f * N : (f + 1) * N] = early(2 * f)
    gate_grad[1] = early(8)
    out_grad[1] = early(10)
    gate_grad[0] = early(12)
    out_grad[0] = early(14)

    wait_all(GAINS, lambda s: gains_all.at[s])
    total = jnp.sum(gains_all[...], axis=0) * scale
    in_gain_grad[...] = total[0:2]
    mid_gain_grad[...] = total[2:4]

    wait_all(ALL_LATE, lambda s: all_late.at[s])
    for f in range(4):
        proj_grad[0, :, f * N : (f + 1) * N] = all_late[4 * f : 4 * f + 4].astype(F32).reshape(N, N) * scale

    wait_sent(TO_CH_0, lambda d: send2.at[0, d])
    wait_sent(TO_ROW_0, lambda d: send1.at[0, d])
    wait_sent(TO_CH_1, lambda d: send2.at[1, d])
    wait_sent(TO_ROW_1, lambda d: send1.at[1, d])
    wait_sent(GRAD_CH_1, lambda d: send1.at[2, d])
    wait_sent(GRAD_ROW_1, lambda d: send2.at[2, d])
    wait_sent(GRAD_CH_0, lambda d: send1.at[3, d])
    wait_sent(GRAD_ROW_0, lambda d: send2.at[3, d])
    wait_sent(SUM_EARLY, lambda d: sum_early_send.at[d])
    wait_sent(ALL_EARLY, lambda d: all_early.at[me])
    wait_sent(SUM_LATE, lambda d: sum_late_send.at[d])
    wait_sent(ALL_LATE, lambda d: all_late.at[me])
    wait_sent(GAINS, lambda d: gains_all.at[me])


def on_device(*arrays):
    layer_f32 = pltpu.VMEM((2, N, CELLS), F32)
    layer_bf16 = pltpu.VMEM((2, N, CELLS), BF16)
    plain_f32 = pltpu.VMEM((N, CELLS), F32)
    return pl.pallas_call(
        kernel,
        out_shape=(
            jax.ShapeDtypeStruct((ROWS, N, N), BF16),
            jax.ShapeDtypeStruct((2, N, 4 * N), F32),
            jax.ShapeDtypeStruct((2, N, N), F32),
            jax.ShapeDtypeStruct((2, N, N), F32),
            jax.ShapeDtypeStruct((2, N), F32),
            jax.ShapeDtypeStruct((2, N), F32),
        ),
        in_specs=[pl.BlockSpec(memory_space=pltpu.VMEM)] * 7,
        out_specs=[pl.BlockSpec(memory_space=pltpu.VMEM)] * 6,
        scratch_shapes=[
            pltpu.VMEM((4, N, WIDE), F32),
            pltpu.VMEM((2, N, 5 * N), BF16),
            pltpu.VMEM((2, 5 * N, N), BF16),
            pltpu.VMEM((2, N, N), BF16),
            plain_f32, plain_f32, plain_f32, plain_f32,
            layer_f32,
            pltpu.VMEM((2, 1, CELLS), F32),
            layer_bf16,
            layer_f32, layer_f32, layer_f32, layer_f32,
            layer_f32, layer_f32, layer_f32,
            pltpu.VMEM((2, 1, CELLS), F32),
            layer_bf16,
            layer_bf16,
            pltpu.VMEM((2, 5 * N, CELLS), BF16),
            pltpu.VMEM((2, N, N), F32),
            pltpu.VMEM((2, N, N), F32),
            pltpu.VMEM((CELLS, N), F32),
            pltpu.VMEM((CELLS, N), F32),
            pltpu.VMEM((2, ROWS, N, N), BF16),
            pltpu.VMEM((2, ROWS, N, N), BF16),
            pltpu.VMEM((4, PEERS, 128, N), BF16),
            pltpu.VMEM((4, PEERS, 128, N), BF16),
            pltpu.VMEM((4, PEERS, 64, N), BF16),
            pltpu.VMEM((4, PEERS, 64, N), BF16),
            pltpu.VMEM((PEERS, 64, N), BF16),
            pltpu.VMEM((PEERS, 64, N), BF16),
            pltpu.VMEM((PEERS, 64, N), BF16),
            pltpu.VMEM((PEERS, 32, N), BF16),
            pltpu.VMEM((PEERS, 32, N), BF16),
            pltpu.VMEM((PEERS, 32, N), BF16),
            pltpu.VMEM((PEERS, 8, N), F32),
            pltpu.SemaphoreType.DMA((PHASES, PEERS)),
            pltpu.SemaphoreType.DMA((PHASES, PEERS)),
        ],
        compiler_params=pltpu.CompilerParams(
            collective_id=0, has_side_effects=True, vmem_limit_bytes=56 * 1024 * 1024
        ),
    )(*arrays)


def solution(mesh):
    return jax.shard_map(
        on_device,
        mesh=mesh,
        in_specs=(
            P(("dp", "pair"), None, None),
            P(("dp", "pair"), None, None),
            P(),
            P(),
            P(),
            P(),
            P(),
        ),
        out_specs=(
            P(("dp", "pair"), None, None),
            P("dp", None, None),
            P("dp", None, None),
            P("dp", None, None),
            P("dp", None),
            P("dp", None),
        ),
        check_vma=False,
    )
```

time: 443 us -> 98.4 us (0.22)
  waiting for transfers between devices: 283 us -> 0 us
  Pallas kernels: 0 us -> 91.9 us
  local copies, waits for them, and re-layouts: 47.7 us -> 5.6 us
  matrix products: 35.4 us -> 0 us
  blocking collectives: 31.1 us -> 0 us
  other arithmetic: 21.5 us -> 0 us
  between operations: 14.4 us -> 0.66 us
  starting transfers between devices: 9.16 us -> 0 us
    psum x1 -> x0, waiting for transfers between devices: 116 us -> none  [on_device(): lax.psum(jnp.stack([projg_out, projg_in]).astype(jnp.bfloat16), 'pair')]
    reduce_scatter x2 -> x0, waiting for transfers between devices: 97.3 us -> none  [the longest x1 56 us: on_device(): lax.psum_scatter(jnp.einsum('ijc,ikc->jkc', window, left_out, preferred_e...]
    pallas_call x0 -> x1, Pallas kernels: none -> 91.9 us  [on_device(): pl.pallas_call(kernel, out_shape=(jax.ShapeDtypeStruct((ROWS, N, N), BF16...]
    all_gather x2 -> x0, waiting for transfers between devices: 61.1 us -> none  [the longest x1 41 us: on_device(): lax.all_gather(right_out, 'pair', axis=0, tiled=True)]
    dot_general x24 -> x0, matrix products: 35.4 us -> none  [the longest x1 5.2 us: on_device(): jnp.einsum('ijc,kjc->kic', grad_prod_in, lax.all_gather(right_in, 'pair',...]
    psum x1 -> x0, blocking collectives: 31.1 us -> none  [on_device(): lax.psum(jnp.stack([ing_out, ing_in]).astype(jnp.bfloat16), 'pair')]
    all_gather x2 -> x0, local copies, waits for them, and re-layouts: 13.3 us -> none  [the longest x1 6.71 us: on_device(): lax.all_gather(right_out, 'pair', axis=0, tiled=True)]
    dot_general x2 -> x0, local copies, waits for them, and re-layouts: 11.4 us -> none  [the longest x1 6.78 us: on_device(): jnp.einsum('ijc,ikc->jkc', window, left_out, preferred_element_type=jnp.f...]
  transfers between devices with their start and end apart: 7 -> 0, of which waited for: 7 -> 0; matrix products, arithmetic and copies ran while one was open for 7% -> 0% of each run, Pallas kernels for 0% -> 0%
where the time goes in v1:
time: 98.4 us; the launch traced here: 98.2 us
  Pallas kernels  91.9 us (93%)
  local copies, waits for them, and re-layouts  5.6 us (6%)
    pallas_call x1, Pallas kernels, on_device(): pl.pallas_call(kernel, out_shape=(jax.ShapeDtypeStruct((ROWS, N, N), BF16...  91.9 us
    unnamed x16, local copies, waits for them, and re-layouts  5.6 us

profile of v1, /device:TPU:1, one launch (start us, length us, event | category | flops | bytes accessed | tf_op | source)
XLA Modules:
  0.0 98.2 jit_solution(4671989296362016067)
XLA Ops:
  0.6 91.9 %shard_map.118 = (bf16[8,128,128]{2,1,0:T(8,128)(2,1)}, f32[2,128,512]{2,1,0:T(8,128)}, f32[2,128,128]{2,1,0:T(8,128)}, f32[2,128,128]{2,1,0:T(8,128)}, f32[2,128]{1,0:T(2,128)}, /*index=5*/f32[2,128]{1,0:T(2,128)}) custom-call(bf16[8,128,128]{2,1,0:T(8,128)(2,1)} %pair_in.1, bf16[8,128,128]{2,1,0:T(8,128)(2,1)} %cotangent.1, f32[2,128]{1,0:T(2,128)} %in_gain.1, ...), custom_call_target="tpu_custom_call" | custom-call | tf_op jit(solution)/shard_map/pallas_call | solution.py:400
  92.6 0.0 copy-start
  92.6 1.7 %copy.19 = bf16[8,128,128]{2,1,0:T(8,128)(2,1)} copy(bf16[8,128,128]{2,1,0:T(8,128)(2,1)} %get-tuple-element.12) | data formatting | bytes 524288
  94.3 0.0 copy-done
  94.3 0.0 copy-start.2
  94.3 0.8 copy.20
  95.1 0.2 copy-done.2
  95.3 0.0 copy-start.1
  95.3 0.7 copy.21
  96.0 0.3 copy-done.1
  96.3 0.0 copy-start.4
  96.3 0.7 copy.22
  96.9 0.0 copy-done.4
  96.9 0.0 copy-start.3
  96.9 0.6 copy.23
  97.5 0.1 copy-done.3
  97.6 0.6 copy.24
Async XLA Ops:
  92.6 1.7 %copy-start = (f32[2,128,512]{2,1,0:T(8,128)S(1)}, f32[2,128,512]{2,1,0:T(8,128)}, u32[]{:S(2)}) copy-start(f32[2,128,512]{2,1,0:T(8,128)} %get-tuple-element.13) | copy-start | bytes 1572868
  94.3 1.0 %copy-start.2 = (f32[2,128,128]{2,1,0:T(8,128)S(1)}, f32[2,128,128]{2,1,0:T(8,128)}, u32[]{:S(2)}) copy-start(f32[2,128,128]{2,1,0:T(8,128)} %get-tuple-element.14) | copy-start | bytes 393220
  95.3 1.0 copy-start.1
  96.3 0.7 copy-start.4
  96.9 0.7 copy-start.3

commit v2 on v1

v2 whole, which is shorter than its diff:
```python
import functools

import jax
import jax.numpy as jnp
from jax import lax
from jax.experimental import pallas as pl
from jax.experimental.pallas import tpu as pltpu
from jax.sharding import PartitionSpec as P

EPSILON = 1e-05
MESH = pl.DeviceIdType.MESH
F32 = jnp.float32
BF16 = jnp.bfloat16

N = 128
PEERS = 16
ROWS = N // PEERS
CELLS = ROWS * N
WIDE = 2 * N
STEPS = CELLS // WIDE
CHUNKS = 2
PER = STEPS // CHUNKS
PART = ROWS * ROWS // CHUNKS

TO_CH_0, TO_ROW_0, TO_CH_1, TO_ROW_1, GRAD_CH_1, GRAD_ROW_1, GRAD_CH_0, GRAD_ROW_0 = range(8)
SUM_EARLY, ALL_EARLY, SUM_LATE, ALL_LATE, GAINS = range(8, 13)
PHASES = 13


def dot(first, second, dims):
    return lax.dot_general(first, second, (dims, ((), ())), preferred_element_type=F32)


def nn(first, second):
    return dot(first, second, ((1,), (0,)))


def nt(first, second):
    return dot(first, second, ((1,), (1,)))


def tn(first, second):
    return dot(first, second, ((0,), (0,)))


def mean_channels(values):
    return jnp.sum(values, axis=0, keepdims=True) * (1.0 / N)


def norm_forward(values):
    shifted = values - mean_channels(values)
    inverse = lax.rsqrt(mean_channels(shifted * shifted) + EPSILON)
    return shifted * inverse, inverse


def norm_backward(scaled, unit, inverse):
    return inverse * (scaled - mean_channels(scaled) - unit * mean_channels(scaled * unit))


def kernel(
    pair_hbm, cot_hbm, in_gain_hbm, proj_weight_hbm, gate_weight_hbm, mid_gain_hbm, out_weight_hbm,
    pair_grad, early_out, late_out, gains_out,
    pair_in, cotangent, in_gain, proj_weight, gate_weight, mid_gain, out_weight,
    gains, weight, weight_t, out_t,
    state0, state1, cot, grad1,
    unit, inverse, normed, sig_l, val_l, sig_r, val_r, gate, output, mix_unit, mix_inverse, mixed,
    go, gp, in_acc, mid_acc,
    turn_a, turn_b, chan_l, chan_r,
    send2, recv2, send1, recv1,
    sum_early_send, sum_early_recv, all_early, sum_late_send, sum_late_recv, all_late, gains_all,
    load_sem, send_sem, recv_sem,
):
    me = lax.axis_index("pair")
    my_x, my_y, my_core = me // 8, (me // 2) % 4, me % 2

    def peer(o):
        x = (my_x + o // 8) % 2
        y = (my_y + (o // 2) % 4) % 4
        core = (my_core + o % 2) % 2
        return x * 8 + y * 2 + core

    barrier = pltpu.get_barrier_semaphore()

    peers = [peer(o) for o in range(PEERS - 1, 0, -1)]
    for target in peers:
        pl.semaphore_signal(barrier, inc=1, device_id={"pair": target}, device_id_type=MESH)

    loads = [
        pltpu.make_async_copy(source, target, load_sem.at[i])
        for i, (source, target) in enumerate((
            (pair_hbm, pair_in), (in_gain_hbm, in_gain), (proj_weight_hbm, proj_weight), (gate_weight_hbm, gate_weight),
            (mid_gain_hbm, mid_gain), (out_weight_hbm, out_weight), (cot_hbm, cotangent),
        ))
    ]
    for load in loads:
        load.start()

    def send_part(phase, h, src_of, dst):
        sem = phase * CHUNKS + h
        for target in peers:
            pltpu.make_async_remote_copy(
                src_ref=src_of(target), dst_ref=dst,
                send_sem=send_sem.at[sem], recv_sem=recv_sem.at[sem],
                device_id={"pair": target}, device_id_type=MESH,
            ).start()

    def wait_part(phase, h, slots):
        fifteen = slots.at[pl.ds(0, PEERS - 1)]
        pltpu.make_async_copy(fifteen, fifteen, recv_sem.at[phase * CHUNKS + h]).wait()

    def wait_sent(phase, h, slots):
        fifteen = slots.at[pl.ds(0, PEERS - 1)]
        pltpu.make_async_copy(fifteen, fifteen, send_sem.at[phase * CHUNKS + h]).wait()

    in_acc[...] = jnp.zeros_like(in_acc)
    mid_acc[...] = jnp.zeros_like(mid_acc)

    def lanes(p):
        return slice(p * WIDE, (p + 1) * WIDE)

    def put_rows(ref, first, values):
        parts = [values[:, i * N : (i + 1) * N].reshape(PEERS, ROWS, N) for i in range(2)]
        ref[:, first : first + 2 * ROWS, :] = jnp.concatenate(parts, axis=1).astype(BF16)

    def get_rows(ref, first):
        block = ref[:, first : first + 2 * ROWS, :].astype(F32)
        return jnp.concatenate([block[:, i * ROWS : (i + 1) * ROWS].reshape(N, N) for i in range(2)], axis=1)

    def project(l, p, state, ref):
        at = lanes(p)
        unit_p, inverse_p = norm_forward(state)
        normed_p = (unit_p * gains[2 * l]).astype(BF16)
        unit[l, :, at] = unit_p
        inverse[l, :, at] = inverse_p
        normed[l, :, at] = normed_p
        projected = nn(weight_t[l], normed_p)
        row = 2 * ROWS * (p % PER)
        sig = jax.nn.sigmoid(projected[0:N])
        val = projected[N : 2 * N]
        sig_l[l, :, at] = sig
        val_l[l, :, at] = val
        put_rows(ref, row, sig * val)
        sig = jax.nn.sigmoid(projected[2 * N : 3 * N])
        val = projected[3 * N : 4 * N]
        sig_r[l, :, at] = sig
        val_r[l, :, at] = val
        put_rows(ref, PART + row, sig * val)
        gate[l, :, at] = jax.nn.sigmoid(projected[4 * N :])

    def steps(h):
        return range(h * PER, (h + 1) * PER)

    def send2_part(slot, phase, h):
        send_part(phase, h, lambda d: send2.at[slot, h, d], recv2.at[slot, h, me])
        recv2[slot, h, me] = send2[slot, h, me]

    def send1_part(slot, phase, h):
        send_part(phase, h, lambda d: send1.at[slot, h, d], recv1.at[slot, h, me])
        recv1[slot, h, me] = send1[slot, h, me]

    def wait2_part(slot, phase, h):
        wait_part(phase, h, recv2.at[slot, h])

    def wait1_part(slot, phase, h):
        wait_part(phase, h, recv1.at[slot, h])

    def part_rows(d, h):
        return slice(d * ROWS * ROWS + h * PART, d * ROWS * ROWS + (h + 1) * PART)

    def channel(c):
        return pl.ds(c, N, stride=ROWS)

    def channel_forward(l, slot2, slot1, phase_in, phase_out):
        for h in range(CHUNKS):
            wait2_part(slot2, phase_in, h)
            for s in range(PEERS):
                turn_a[part_rows(s, h), :] = recv2[slot2, h, s, :PART].astype(F32)
                turn_b[part_rows(s, h), :] = recv2[slot2, h, s, PART:].astype(F32)
        for c in range(ROWS):
            left = turn_a[channel(c), :].astype(BF16)
            right = turn_b[channel(c), :].astype(BF16)
            chan_l[l, c] = left
            chan_r[l, c] = right
            turn_a[channel(c), :] = nt(left, right) if l == 0 else tn(left, right)
        for h in range(CHUNKS):
            for d in range(PEERS):
                send1[slot1, h, d] = turn_a[part_rows(d, h), :].astype(BF16)
            send1_part(slot1, phase_out, h)

    def channel_backward(l, slot1, slot2, phase_in, phase_out):
        for h in range(CHUNKS):
            wait1_part(slot1, phase_in, h)
            for s in range(PEERS):
                turn_a[part_rows(s, h), :] = recv1[slot1, h, s].astype(F32)
        for c in range(ROWS):
            grad = turn_a[channel(c), :].astype(BF16)
            left, right = chan_l[l, c], chan_r[l, c]
            turn_a[channel(c), :] = nn(grad, right) if l == 0 else nt(right, grad)
            turn_b[channel(c), :] = tn(grad, left) if l == 0 else nn(left, grad)
        for h in range(CHUNKS):
            for d in range(PEERS):
                send2[slot2, h, d, :PART] = turn_a[part_rows(d, h), :].astype(BF16)
                send2[slot2, h, d, PART:] = turn_b[part_rows(d, h), :].astype(BF16)
            send2_part(slot2, phase_out, h)

    def finish(l, p, product):
        at = lanes(p)
        mix_unit_p, mix_inverse_p = norm_forward(product)
        mixed_p = (mix_unit_p * gains[2 * l + 1]).astype(BF16)
        mix_unit[l, :, at] = mix_unit_p
        mix_inverse[l, :, at] = mix_inverse_p
        mixed[l, :, at] = mixed_p
        output_p = nn(out_t[l], mixed_p)
        output[l, :, at] = output_p
        return output_p

    def fold(values):
        return values[:, :N] + values[:, N:]

    def back_head(l, p, gradient, ref):
        at = lanes(p)
        gate_p = gate[l, :, at]
        go_p = (gradient * gate_p).astype(BF16)
        go[l, :, at] = go_p
        gp[l, 4 * N :, at] = (gradient * output[l, :, at] * gate_p * (1.0 - gate_p)).astype(BF16)
        grad_mixed = nn(out_weight[l], go_p)
        mix_unit_p = mix_unit[l, :, at]
        mid_acc[l] += fold(grad_mixed * mix_unit_p)
        grad_product = norm_backward(grad_mixed * gains[2 * l + 1], mix_unit_p, mix_inverse[l, :, at])
        put_rows(ref, 2 * ROWS * (p % PER), grad_product)

    def back_pieces(l, p, ref):
        at = lanes(p)
        row = 2 * ROWS * (p % PER)
        sig = sig_l[l, :, at]
        plain = get_rows(ref, row) * sig
        gp[l, 0:N, at] = (plain * val_l[l, :, at] * (1.0 - sig)).astype(BF16)
        gp[l, N : 2 * N, at] = plain.astype(BF16)
        sig = sig_r[l, :, at]
        plain = get_rows(ref, PART + row) * sig
        gp[l, 2 * N : 3 * N, at] = (plain * val_r[l, :, at] * (1.0 - sig)).astype(BF16)
        gp[l, 3 * N : 4 * N, at] = plain.astype(BF16)

    def back_tail(l, p, gradient):
        at = lanes(p)
        grad_normed = nn(weight[l], gp[l, :, at])
        unit_p = unit[l, :, at]
        in_acc[l] += fold(grad_normed * unit_p)
        return gradient + norm_backward(grad_normed * gains[2 * l], unit_p, inverse[l, :, at])

    loads[0].wait()
    for a in range(ROWS):
        state0[:, a * N : (a + 1) * N] = pair_in[a].astype(F32).T
    for load in loads[1:4]:
        load.wait()

    def set_gain(index, source, l):
        row = jnp.broadcast_to(source[l : l + 1, :], (N, N)).T
        gains[index] = jnp.concatenate([row, row], axis=1)

    def set_weights(l):
        set_gain(2 * l, in_gain, l)
        for f in range(4):
            block = proj_weight[l, :, f * N : (f + 1) * N]
            weight[l, :, f * N : (f + 1) * N] = block
            weight_t[l, f * N : (f + 1) * N, :] = block.astype(F32).T.astype(BF16)
        weight[l, :, 4 * N :] = gate_weight[l]
        weight_t[l, 4 * N :, :] = gate_weight[l].astype(F32).T.astype(BF16)

    set_weights(0)
    for h in range(CHUNKS):
        for p in steps(h):
            project(0, p, state0[:, lanes(p)], send2.at[0, h])
        if h == 0:
            pl.semaphore_wait(barrier, PEERS - 1)
        send2_part(0, TO_CH_0, h)

    for load in loads[4:]:
        load.wait()
    set_weights(1)
    for l in range(2):
        set_gain(2 * l + 1, mid_gain, l)
        out_t[l] = out_weight[l].astype(F32).T.astype(BF16)
    for a in range(ROWS):
        cot[:, a * N : (a + 1) * N] = cotangent[a].astype(F32).T

    channel_forward(0, 0, 0, TO_CH_0, TO_ROW_0)

    for h in range(CHUNKS):
        wait1_part(0, TO_ROW_0, h)
        for p in steps(h):
            at = lanes(p)
            output_p = finish(0, p, get_rows(recv1.at[0, h], 2 * ROWS * (p % PER)))
            state = (state0[:, at] + gate[0, :, at] * output_p).astype(BF16).astype(F32)
            state1[:, at] = state
            project(1, p, state, send2.at[1, h])
        send2_part(1, TO_CH_1, h)

    channel_forward(1, 1, 1, TO_CH_1, TO_ROW_1)

    for h in range(CHUNKS):
        wait1_part(1, TO_ROW_1, h)
        for p in steps(h):
            finish(1, p, get_rows(recv1.at[1, h], 2 * ROWS * (p % PER)))
            back_head(1, p, cot[:, lanes(p)], send1.at[2, h])
        send1_part(2, GRAD_CH_1, h)

    channel_backward(1, 2, 2, GRAD_CH_1, GRAD_ROW_1)

    for h in range(CHUNKS):
        wait2_part(2, GRAD_ROW_1, h)
        for p in steps(h):
            at = lanes(p)
            back_pieces(1, p, recv2.at[2, h])
            gradient = back_tail(1, p, cot[:, at])
            grad1[:, at] = gradient
            back_head(0, p, gradient, send1.at[3, h])
        send1_part(3, GRAD_CH_0, h)

    def put_early(first, values):
        for i in range(N // 64):
            sum_early_send[first + i] = values[64 * i : 64 * i + 64, :].astype(BF16)

    for f in range(5):
        put_early(2 * f, nt(normed[1], gp[1, f * N : (f + 1) * N, :]))
    put_early(10, nt(mixed[1], go[1]))
    put_early(12, nt(normed[0], gp[0, 4 * N :, :]))
    put_early(14, nt(mixed[0], go[0]))
    send_part(SUM_EARLY, 0, lambda d: sum_early_send.at[d], sum_early_recv.at[me])
    sum_early_recv[me] = sum_early_send[me]

    channel_backward(0, 3, 3, GRAD_CH_0, GRAD_ROW_0)

    wait_part(SUM_EARLY, 0, sum_early_recv)
    all_early[me] = jnp.sum(sum_early_recv[...].astype(F32), axis=0).astype(BF16)
    send_part(ALL_EARLY, 0, lambda d: all_early.at[me], all_early.at[me])

    def last_rows(p):
        gradient = back_tail(0, p, grad1[:, lanes(p)])
        for i in range(2):
            pair_grad[2 * p + i] = gradient[:, i * N : (i + 1) * N].T.astype(BF16)

    for h in range(CHUNKS):
        wait2_part(3, GRAD_ROW_0, h)
        for p in steps(h):
            back_pieces(0, p, recv2.at[3, h])
        if h < CHUNKS - 1:
            for p in steps(h):
                last_rows(p)

    for f in range(4):
        values = nt(normed[0], gp[0, f * N : (f + 1) * N, :])
        for i in range(4):
            sum_late_send[4 * f + i] = values[32 * i : 32 * i + 32, :].astype(BF16)
    send_part(SUM_LATE, 0, lambda d: sum_late_send.at[d], sum_late_recv.at[me])
    sum_late_recv[me] = sum_late_send[me]

    for p in steps(CHUNKS - 1):
        last_rows(p)

    gain_rows = [jnp.sum(ref[l].T, axis=0, keepdims=True) for ref in (in_acc, mid_acc) for l in range(2)]
    gains_all[me] = jnp.concatenate(gain_rows + [jnp.zeros((4, N), F32)], axis=0)
    send_part(GAINS, 0, lambda d: gains_all.at[me], gains_all.at[me])

    wait_part(SUM_LATE, 0, sum_late_recv)
    all_late[me] = jnp.sum(sum_late_recv[...].astype(F32), axis=0).astype(BF16)
    send_part(ALL_LATE, 0, lambda d: all_late.at[me], all_late.at[me])

    wait_part(ALL_EARLY, 0, all_early)
    early_out[...] = all_early[...]
    for h in range(CHUNKS):
        for slot, two, one in ((0, TO_CH_0, TO_ROW_0), (1, TO_CH_1, TO_ROW_1), (2, GRAD_ROW_1, GRAD_CH_1), (3, GRAD_ROW_0, GRAD_CH_0)):
            wait_sent(two, h, send2.at[slot, h])
            wait_sent(one, h, send1.at[slot, h])
    wait_sent(SUM_EARLY, 0, sum_early_send)
    wait_sent(ALL_EARLY, 0, all_early)
    wait_sent(SUM_LATE, 0, sum_late_send)
    wait_sent(GAINS, 0, gains_all)

    wait_part(GAINS, 0, gains_all)
    gains_out[...] = jnp.sum(gains_all[...], axis=0)

    wait_part(ALL_LATE, 0, all_late)
    late_out[...] = all_late[...]
    wait_sent(ALL_LATE, 0, all_late)


def write_kernel(
    pair, early_in, late_in, gains_in,
    pair_grad, proj_grad, gate_grad, out_grad, in_gain_grad, mid_gain_grad,
):
    scale = 1.0 / N
    pair_grad[...] = pair[...]

    def early(first):
        return early_in[first : first + 2].astype(F32).reshape(N, N) * scale

    for f in range(4):
        proj_grad[0, :, f * N : (f + 1) * N] = late_in[4 * f : 4 * f + 4].astype(F32).reshape(N, N) * scale
        proj_grad[1, :, f * N : (f + 1) * N] = early(2 * f)
    gate_grad[1] = early(8)
    out_grad[1] = early(10)
    gate_grad[0] = early(12)
    out_grad[0] = early(14)
    in_gain_grad[...] = gains_in[0:2, :] * scale
    mid_gain_grad[...] = gains_in[2:4, :] * scale


def on_device(*arrays):
    layer_f32 = pltpu.VMEM((2, N, CELLS), F32)
    layer_bf16 = pltpu.VMEM((2, N, CELLS), BF16)
    plain_f32 = pltpu.VMEM((N, CELLS), F32)
    vmem = pl.BlockSpec(memory_space=pltpu.VMEM)
    results = pl.pallas_call(
        kernel,
        out_shape=(
            jax.ShapeDtypeStruct((ROWS, N, N), BF16),
            jax.ShapeDtypeStruct((PEERS, 64, N), BF16),
            jax.ShapeDtypeStruct((PEERS, 32, N), BF16),
            jax.ShapeDtypeStruct((8, N), F32),
        ),
        in_specs=[pl.BlockSpec(memory_space=pl.ANY)] * 7,
        out_specs=[vmem] * 4,
        scratch_shapes=[pltpu.VMEM(array.shape, array.dtype) for array in arrays] + [
            pltpu.VMEM((4, N, WIDE), F32),
            pltpu.VMEM((2, N, 5 * N), BF16),
            pltpu.VMEM((2, 5 * N, N), BF16),
            pltpu.VMEM((2, N, N), BF16),
            plain_f32, plain_f32, plain_f32, plain_f32,
            layer_f32,
            pltpu.VMEM((2, 1, CELLS), F32),
            layer_bf16,
            layer_f32, layer_f32, layer_f32, layer_f32,
            layer_f32, layer_f32, layer_f32,
            pltpu.VMEM((2, 1, CELLS), F32),
            layer_bf16,
            layer_bf16,
            pltpu.VMEM((2, 5 * N, CELLS), BF16),
            pltpu.VMEM((2, N, N), F32),
            pltpu.VMEM((2, N, N), F32),
            pltpu.VMEM((CELLS, N), F32),
            pltpu.VMEM((CELLS, N), F32),
            pltpu.VMEM((2, ROWS, N, N), BF16),
            pltpu.VMEM((2, ROWS, N, N), BF16),
            pltpu.VMEM((4, CHUNKS, PEERS, 2 * PART, N), BF16),
            pltpu.VMEM((4, CHUNKS, PEERS, 2 * PART, N), BF16),
            pltpu.VMEM((4, CHUNKS, PEERS, PART, N), BF16),
            pltpu.VMEM((4, CHUNKS, PEERS, PART, N), BF16),
            pltpu.VMEM((PEERS, 64, N), BF16),
            pltpu.VMEM((PEERS, 64, N), BF16),
            pltpu.VMEM((PEERS, 64, N), BF16),
            pltpu.VMEM((PEERS, 32, N), BF16),
            pltpu.VMEM((PEERS, 32, N), BF16),
            pltpu.VMEM((PEERS, 32, N), BF16),
            pltpu.VMEM((PEERS, 8, N), F32),
            pltpu.SemaphoreType.DMA((7,)),
            pltpu.SemaphoreType.DMA((PHASES * CHUNKS,)),
            pltpu.SemaphoreType.DMA((PHASES * CHUNKS,)),
        ],
        compiler_params=pltpu.CompilerParams(
            collective_id=0, has_side_effects=True, vmem_limit_bytes=56 * 1024 * 1024
        ),
    )(*arrays)
    return pl.pallas_call(
        write_kernel,
        out_shape=(
            jax.ShapeDtypeStruct((ROWS, N, N), BF16),
            jax.ShapeDtypeStruct((2, N, 4 * N), F32),
            jax.ShapeDtypeStruct((2, N, N), F32),
            jax.ShapeDtypeStruct((2, N, N), F32),
            jax.ShapeDtypeStruct((2, N), F32),
            jax.ShapeDtypeStruct((2, N), F32),
        ),
        in_specs=[vmem] * 4,
        out_specs=[vmem] * 6,
    )(*results)


def solution(mesh):
    return jax.shard_map(
        on_device,
        mesh=mesh,
        in_specs=(
            P(("dp", "pair"), None, None),
            P(("dp", "pair"), None, None),
            P(),
            P(),
            P(),
            P(),
            P(),
        ),
        out_specs=(
            P(("dp", "pair"), None, None),
            P("dp", None, None),
            P("dp", None, None),
            P("dp", None, None),
            P("dp", None),
            P("dp", None),
        ),
        check_vma=False,
    )
```

time: 98.4 us -> 75 us (0.76)
  Pallas kernels: 91.9 us -> 74.2 us
  local copies, waits for them, and re-layouts: 5.6 us -> 0 us
    pallas_call x1, Pallas kernels: 91.9 us -> 72.1 us  [on_device(): pl.pallas_call(kernel, out_shape=(jax.ShapeDtypeStruct((ROWS, N, N), BF16...]
    unnamed x16 -> x0, local copies, waits for them, and re-layouts: 5.6 us -> none
    pallas_call x0 -> x1, Pallas kernels: none -> 2.1 us  [on_device(): pl.pallas_call(write_kernel, out_shape=(jax.ShapeDtypeStruct((ROWS, N, N)...]
where the time goes in v2:
time: 75 us; the launch traced here: 74.9 us
  Pallas kernels  74.2 us (99%)
    pallas_call x1, Pallas kernels, on_device(): pl.pallas_call(kernel, out_shape=(jax.ShapeDtypeStruct((ROWS, N, N), BF16...  72.1 us
    pallas_call x1, Pallas kernels, on_device(): pl.pallas_call(write_kernel, out_shape=(jax.ShapeDtypeStruct((ROWS, N, N)...  2.1 us

profile of v2, /device:TPU:1, one launch (start us, length us, event | category | flops | bytes accessed | tf_op | source)
XLA Modules:
  0.0 74.9 jit_solution(9436327175999692495)
XLA Ops:
  0.6 72.1 %shard_map.118 = (bf16[8,128,128]{2,1,0:T(8,128)(2,1)}, bf16[16,64,128]{2,1,0:T(8,128)(2,1)}, bf16[16,32,128]{2,1,0:T(8,128)(2,1)}, f32[8,128]{1,0:T(8,128)}) custom-call(bf16[8,128,128]{2,1,0:T(8,128)(2,1)} %pair_hbm.1, bf16[8,128,128]{2,1,0:T(8,128)(2,1)} %cot_hbm.1, f32[2,128]{1,0:T(2,128)} %in_gain_hbm.1, bf16[2,128,512]{2,1,0:T(8,128)(2,1)} %proj_weight_hbm.1, ...), custom_call_target="tpu_custom_call" | custom-call | tf_op jit(solution)/shard_map/pallas_call | solution.py:414
  72.8 2.1 %shard_map.119 = (bf16[8,128,128]{2,1,0:T(8,128)(2,1)}, f32[2,128,512]{2,1,0:T(8,128)}, f32[2,128,128]{2,1,0:T(8,128)}, f32[2,128,128]{2,1,0:T(8,128)}, f32[2,128]{1,0:T(2,128)}, /*index=5*/f32[2,128]{1,0:T(2,128)}) custom-call(bf16[8,128,128]{2,1,0:T(8,128)(2,1)} %get-tuple-element.10.pair, bf16[16,64,128]{2,1,0:T(8,128)(2,1)} %get-tuple-element.11.early_in, ...), custom_call_target="tpu_custom_call" | custom-call | tf_op jit(solution)/shard_map/pallas_call | solution.py:464

commit v3 on v2

--- a/solution.py
+++ b/solution.py
@@ -41,6 +41,10 @@
 
 def tn(first, second):
     return dot(first, second, ((0,), (0,)))
+
+
+def sigmoid(values):
+    return 0.5 * jnp.tanh(0.5 * values) + 0.5
 
 
 def mean_channels(values):
@@ -81,7 +85,7 @@
 
     barrier = pltpu.get_barrier_semaphore()
 
-    peers = [peer(o) for o in range(PEERS - 1, 0, -1)]
+    peers = [peer(o) for o in (12, 4, 13, 5, 10, 2, 14, 6, 11, 3, 15, 7, 8, 9, 1)]
     for target in peers:
         pl.semaphore_signal(barrier, inc=1, device_id={"pair": target}, device_id_type=MESH)
 
@@ -135,17 +139,17 @@
         normed[l, :, at] = normed_p
         projected = nn(weight_t[l], normed_p)
         row = 2 * ROWS * (p % PER)
-        sig = jax.nn.sigmoid(projected[0:N])
+        sig = sigmoid(projected[0:N])
         val = projected[N : 2 * N]
         sig_l[l, :, at] = sig
         val_l[l, :, at] = val
         put_rows(ref, row, sig * val)
-        sig = jax.nn.sigmoid(projected[2 * N : 3 * N])
+        sig = sigmoid(projected[2 * N : 3 * N])
         val = projected[3 * N : 4 * N]
         sig_r[l, :, at] = sig
         val_r[l, :, at] = val
         put_rows(ref, PART + row, sig * val)
-        gate[l, :, at] = jax.nn.sigmoid(projected[4 * N :])
+        gate[l, :, at] = sigmoid(projected[4 * N :])
 
     def steps(h):
         return range(h * PER, (h + 1) * PER)
@@ -414,10 +418,10 @@
     results = pl.pallas_call(
         kernel,
         out_shape=(
-            jax.ShapeDtypeStruct((ROWS, N, N), BF16),
-            jax.ShapeDtypeStruct((PEERS, 64, N), BF16),
-            jax.ShapeDtypeStruct((PEERS, 32, N), BF16),
-            jax.ShapeDtypeStruct((8, N), F32),
+            pltpu.VMEM((ROWS, N, N), BF16),
+            pltpu.VMEM((PEERS, 64, N), BF16),
+            pltpu.VMEM((PEERS, 32, N), BF16),
+            pltpu.VMEM((8, N), F32),
         ),
         in_specs=[pl.BlockSpec(memory_space=pl.ANY)] * 7,
         out_specs=[vmem] * 4,
@@ -473,6 +477,7 @@
         ),
         in_specs=[vmem] * 4,
         out_specs=[vmem] * 6,
+        compiler_params=pltpu.CompilerParams(vmem_limit_bytes=4 * 1024 * 1024),
     )(*results)
 
 

time: 75 us -> 71.4 us (0.952)
  Pallas kernels: 74.2 us -> 70.6 us
    pallas_call x1, Pallas kernels: 72.1 us -> 69.6 us  [on_device(): pl.pallas_call(kernel, out_shape=(pltpu.VMEM((ROWS, N, N), BF16), pltpu.V...]
    pallas_call x1, Pallas kernels: 2.1 us -> 1.04 us  [on_device(): pl.pallas_call(write_kernel, out_shape=(jax.ShapeDtypeStruct((ROWS, N, N)...]
where the time goes in v3:
time: 71.4 us; the launch traced here: 71.2 us
  Pallas kernels  70.6 us (99%)
    pallas_call x1, Pallas kernels, on_device(): pl.pallas_call(kernel, out_shape=(pltpu.VMEM((ROWS, N, N), BF16), pltpu.V...  69.6 us

profile of v3, /device:TPU:1, one launch (start us, length us, event | category | flops | bytes accessed | tf_op | source)
XLA Modules:
  0.0 71.2 jit_solution(8820774614692845259)
XLA Ops:
  0.6 69.6 %shard_map.118 = (bf16[8,128,128]{2,1,0:T(8,128)(2,1)S(1)}, bf16[16,64,128]{2,1,0:T(8,128)(2,1)S(1)}, bf16[16,32,128]{2,1,0:T(8,128)(2,1)S(1)}, f32[8,128]{1,0:T(8,128)S(1)}) custom-call(bf16[8,128,128]{2,1,0:T(8,128)(2,1)} %pair_hbm.1, bf16[8,128,128]{2,1,0:T(8,128)(2,1)} %cot_hbm.1, f32[2,128]{1,0:T(2,128)} %in_gain_hbm.1, ...), custom_call_target="tpu_custom_call" | custom-call | tf_op jit(solution)/shard_map/pallas_call | solution.py:418
  70.2 1.0 %shard_map.119 = (bf16[8,128,128]{2,1,0:T(8,128)(2,1)}, f32[2,128,512]{2,1,0:T(8,128)}, f32[2,128,128]{2,1,0:T(8,128)}, f32[2,128,128]{2,1,0:T(8,128)}, f32[2,128]{1,0:T(2,128)}, /*index=5*/f32[2,128]{1,0:T(2,128)}) custom-call(bf16[8,128,128]{2,1,0:T(8,128)(2,1)S(1)} %get-tuple-element.10.pair, bf16[16,64,128]{2,1,0:T(8,128)(2,1)S(1)} %get-tuple-element.11.early_in, ...), custom_call_target="tpu_custom_call" | custom-call | tf_op jit(solution)/shard_map/pallas_call | solution.py:468

commit v4 on v3

--- a/solution.py
+++ b/solution.py
@@ -66,8 +66,9 @@
     pair_grad, early_out, late_out, gains_out,
     pair_in, cotangent, in_gain, proj_weight, gate_weight, mid_gain, out_weight,
     gains, weight, weight_t, out_t,
-    state0, state1, cot, grad1,
-    unit, inverse, normed, sig_l, val_l, sig_r, val_r, gate, output, mix_unit, mix_inverse, mixed,
+    state0, cot, grad1,
+    unit, inverse, normed, sig_l, val_l, sig_r, val_r, gate, gate_der, output, mix_unit, mix_inverse, mixed,
+    grad_mixed, scaled, scaled_mean, grad_normed,
     go, gp, in_acc, mid_acc,
     turn_a, turn_b, chan_l, chan_r,
     send2, recv2, send1, recv1,
@@ -85,7 +86,7 @@
 
     barrier = pltpu.get_barrier_semaphore()
 
-    peers = [peer(o) for o in (12, 4, 13, 5, 10, 2, 14, 6, 11, 3, 15, 7, 8, 9, 1)]
+    peers = [peer(o) for o in (4, 12, 5, 13, 2, 10, 6, 14, 3, 11, 7, 15, 8, 9, 1)]
     for target in peers:
         pl.semaphore_signal(barrier, inc=1, device_id={"pair": target}, device_id_type=MESH)
 
@@ -149,7 +150,27 @@
         sig_r[l, :, at] = sig
         val_r[l, :, at] = val
         put_rows(ref, PART + row, sig * val)
-        gate[l, :, at] = sigmoid(projected[4 * N :])
+        gate[l, :, at] = projected[4 * N :]
+
+    def after_project(l):
+        for p in range(STEPS):
+            at = lanes(p)
+            gate_p = sigmoid(gate[l, :, at])
+            gate[l, :, at] = gate_p
+            for sig, val in ((sig_l, val_l), (sig_r, val_r)):
+                sig_p = sig[l, :, at]
+                val[l, :, at] = val[l, :, at] * sig_p * (1.0 - sig_p)
+            if l == 1:
+                gate_der[0, :, at] = output[:, at] * gate[0, :, at] * (1.0 - gate[0, :, at])
+                cot_p = cot[:, at]
+                gate_der[1, :, at] = cot_p * gate_p * (1.0 - gate_p)
+                go_p = (cot_p * gate_p).astype(BF16)
+                go[1, :, at] = go_p
+                grad_mixed_p = nn(out_weight[1], go_p)
+                grad_mixed[:, at] = grad_mixed_p
+                scaled_p = grad_mixed_p * gains[3]
+                scaled[:, at] = scaled_p
+                scaled_mean[:, at] = mean_channels(scaled_p)
 
     def steps(h):
         return range(h * PER, (h + 1) * PER)
@@ -207,50 +228,27 @@
                 send2[slot2, h, d, PART:] = turn_b[part_rows(d, h), :].astype(BF16)
             send2_part(slot2, phase_out, h)
 
-    def finish(l, p, product):
-        at = lanes(p)
-        mix_unit_p, mix_inverse_p = norm_forward(product)
-        mixed_p = (mix_unit_p * gains[2 * l + 1]).astype(BF16)
-        mix_unit[l, :, at] = mix_unit_p
-        mix_inverse[l, :, at] = mix_inverse_p
-        mixed[l, :, at] = mixed_p
-        output_p = nn(out_t[l], mixed_p)
-        output[l, :, at] = output_p
-        return output_p
-
     def fold(values):
         return values[:, :N] + values[:, N:]
-
-    def back_head(l, p, gradient, ref):
-        at = lanes(p)
-        gate_p = gate[l, :, at]
-        go_p = (gradient * gate_p).astype(BF16)
-        go[l, :, at] = go_p
-        gp[l, 4 * N :, at] = (gradient * output[l, :, at] * gate_p * (1.0 - gate_p)).astype(BF16)
-        grad_mixed = nn(out_weight[l], go_p)
-        mix_unit_p = mix_unit[l, :, at]
-        mid_acc[l] += fold(grad_mixed * mix_unit_p)
-        grad_product = norm_backward(grad_mixed * gains[2 * l + 1], mix_unit_p, mix_inverse[l, :, at])
-        put_rows(ref, 2 * ROWS * (p % PER), grad_product)
 
     def back_pieces(l, p, ref):
         at = lanes(p)
         row = 2 * ROWS * (p % PER)
-        sig = sig_l[l, :, at]
-        plain = get_rows(ref, row) * sig
-        gp[l, 0:N, at] = (plain * val_l[l, :, at] * (1.0 - sig)).astype(BF16)
-        gp[l, N : 2 * N, at] = plain.astype(BF16)
-        sig = sig_r[l, :, at]
-        plain = get_rows(ref, PART + row) * sig
-        gp[l, 2 * N : 3 * N, at] = (plain * val_r[l, :, at] * (1.0 - sig)).astype(BF16)
-        gp[l, 3 * N : 4 * N, at] = plain.astype(BF16)
+        for side, (sig, val) in enumerate(((sig_l, val_l), (sig_r, val_r))):
+            grad = get_rows(ref, side * PART + row)
+            first = 2 * N * side
+            gp[l, first : first + N, at] = (grad * val[l, :, at]).astype(BF16)
+            gp[l, first + N : first + 2 * N, at] = (grad * sig[l, :, at]).astype(BF16)
 
     def back_tail(l, p, gradient):
         at = lanes(p)
-        grad_normed = nn(weight[l], gp[l, :, at])
+        grad_normed_p = nn(weight[l], gp[l, :, at])
         unit_p = unit[l, :, at]
-        in_acc[l] += fold(grad_normed * unit_p)
-        return gradient + norm_backward(grad_normed * gains[2 * l], unit_p, inverse[l, :, at])
+        if l == 1:
+            grad_normed[:, at] = grad_normed_p
+        else:
+            in_acc[l] += fold(grad_normed_p * unit_p)
+        return gradient + norm_backward(grad_normed_p * gains[2 * l], unit_p, inverse[l, :, at])
 
     loads[0].wait()
     for a in range(ROWS):
@@ -288,26 +286,48 @@
     for a in range(ROWS):
         cot[:, a * N : (a + 1) * N] = cotangent[a].astype(F32).T
 
+    after_project(0)
+
     channel_forward(0, 0, 0, TO_CH_0, TO_ROW_0)
 
     for h in range(CHUNKS):
         wait1_part(0, TO_ROW_0, h)
         for p in steps(h):
             at = lanes(p)
-            output_p = finish(0, p, get_rows(recv1.at[0, h], 2 * ROWS * (p % PER)))
+            mix_unit_p, mix_inverse_p = norm_forward(get_rows(recv1.at[0, h], 2 * ROWS * (p % PER)))
+            mixed_p = (mix_unit_p * gains[1]).astype(BF16)
+            mix_unit[0, :, at] = mix_unit_p
+            mix_inverse[:, at] = mix_inverse_p
+            mixed[0, :, at] = mixed_p
+            output_p = nn(out_t[0], mixed_p)
+            output[:, at] = output_p
             state = (state0[:, at] + gate[0, :, at] * output_p).astype(BF16).astype(F32)
-            state1[:, at] = state
             project(1, p, state, send2.at[1, h])
         send2_part(1, TO_CH_1, h)
 
+    after_project(1)
+
     channel_forward(1, 1, 1, TO_CH_1, TO_ROW_1)
 
     for h in range(CHUNKS):
         wait1_part(1, TO_ROW_1, h)
         for p in steps(h):
-            finish(1, p, get_rows(recv1.at[1, h], 2 * ROWS * (p % PER)))
-            back_head(1, p, cot[:, lanes(p)], send1.at[2, h])
+            at = lanes(p)
+            row = 2 * ROWS * (p % PER)
+            mix_unit_p, mix_inverse_p = norm_forward(get_rows(recv1.at[1, h], row))
+            mix_unit[1, :, at] = mix_unit_p
+            scaled_p = scaled[:, at]
+            mean_two = mean_channels(scaled_p * mix_unit_p)
+            put_rows(send1.at[2, h], row, mix_inverse_p * (scaled_p - scaled_mean[:, at] - mix_unit_p * mean_two))
         send1_part(2, GRAD_CH_1, h)
+
+    for p in range(STEPS):
+        at = lanes(p)
+        mix_unit_p = mix_unit[1, :, at]
+        mixed_p = (mix_unit_p * gains[3]).astype(BF16)
+        mixed[1, :, at] = mixed_p
+        gp[1, 4 * N :, at] = (gate_der[1, :, at] * nn(out_t[1], mixed_p)).astype(BF16)
+        mid_acc[1] += fold(grad_mixed[:, at] * mix_unit_p)
 
     channel_backward(1, 2, 2, GRAD_CH_1, GRAD_ROW_1)
 
@@ -318,8 +338,19 @@
             back_pieces(1, p, recv2.at[2, h])
             gradient = back_tail(1, p, cot[:, at])
             grad1[:, at] = gradient
-            back_head(0, p, gradient, send1.at[3, h])
+            go_p = (gradient * gate[0, :, at]).astype(BF16)
+            go[0, :, at] = go_p
+            grad_mixed_p = nn(out_weight[0], go_p)
+            grad_mixed[:, at] = grad_mixed_p
+            grad_product = norm_backward(grad_mixed_p * gains[1], mix_unit[0, :, at], mix_inverse[:, at])
+            put_rows(send1.at[3, h], 2 * ROWS * (p % PER), grad_product)
         send1_part(3, GRAD_CH_0, h)
+
+    for p in range(STEPS):
+        at = lanes(p)
+        gp[0, 4 * N :, at] = (grad1[:, at] * gate_der[0, :, at]).astype(BF16)
+        mid_acc[0] += fold(grad_mixed[:, at] * mix_unit[0, :, at])
+        in_acc[1] += fold(grad_normed[:, at] * unit[1, :, at])
 
     def put_early(first, values):
         for i in range(N // 64):
@@ -330,6 +361,8 @@
     put_early(10, nt(mixed[1], go[1]))
     put_early(12, nt(normed[0], gp[0, 4 * N :, :]))
     put_early(14, nt(mixed[0], go[0]))
+    for h in range(CHUNKS):
+        wait_sent(GRAD_CH_0, h, send1.at[3, h])
     send_part(SUM_EARLY, 0, lambda d: sum_early_send.at[d], sum_early_recv.at[me])
     sum_early_recv[me] = sum_early_send[me]
 
@@ -337,6 +370,8 @@
 
     wait_part(SUM_EARLY, 0, sum_early_recv)
     all_early[me] = jnp.sum(sum_early_recv[...].astype(F32), axis=0).astype(BF16)
+    for h in range(CHUNKS):
+        wait_sent(GRAD_ROW_0, h, send2.at[3, h])
     send_part(ALL_EARLY, 0, lambda d: all_early.at[me], all_early.at[me])
 
     def last_rows(p):
@@ -373,7 +408,7 @@
     wait_part(ALL_EARLY, 0, all_early)
     early_out[...] = all_early[...]
     for h in range(CHUNKS):
-        for slot, two, one in ((0, TO_CH_0, TO_ROW_0), (1, TO_CH_1, TO_ROW_1), (2, GRAD_ROW_1, GRAD_CH_1), (3, GRAD_ROW_0, GRAD_CH_0)):
+        for slot, two, one in ((0, TO_CH_0, TO_ROW_0), (1, TO_CH_1, TO_ROW_1), (2, GRAD_ROW_1, GRAD_CH_1)):
             wait_sent(two, h, send2.at[slot, h])
             wait_sent(one, h, send1.at[slot, h])
     wait_sent(SUM_EARLY, 0, sum_early_send)
@@ -430,14 +465,17 @@
             pltpu.VMEM((2, N, 5 * N), BF16),
             pltpu.VMEM((2, 5 * N, N), BF16),
             pltpu.VMEM((2, N, N), BF16),
-            plain_f32, plain_f32, plain_f32, plain_f32,
+            plain_f32, plain_f32, plain_f32,
             layer_f32,
             pltpu.VMEM((2, 1, CELLS), F32),
             layer_bf16,
             layer_f32, layer_f32, layer_f32, layer_f32,
-            layer_f32, layer_f32, layer_f32,
-            pltpu.VMEM((2, 1, CELLS), F32),
+            layer_f32, layer_f32, plain_f32, layer_f32,
+            pltpu.VMEM((1, CELLS), F32),
             layer_bf16,
+            plain_f32, plain_f32,
+            pltpu.VMEM((1, CELLS), F32),
+            plain_f32,
             layer_bf16,
             pltpu.VMEM((2, 5 * N, CELLS), BF16),
             pltpu.VMEM((2, N, N), F32),

time: 71.4 us -> 70 us (0.980)
  Pallas kernels: 70.6 us -> 69.2 us
    pallas_call x1, Pallas kernels: 69.6 us -> 68.1 us  [on_device(): pl.pallas_call(kernel, out_shape=(pltpu.VMEM((ROWS, N, N), BF16), pltpu.V...]
where the time goes in v4:
time: 70 us; the launch traced here: 69.8 us
  Pallas kernels  69.2 us (99%)
    pallas_call x1, Pallas kernels, on_device(): pl.pallas_call(kernel, out_shape=(pltpu.VMEM((ROWS, N, N), BF16), pltpu.V...  68.1 us

profile of v4, /device:TPU:1, one launch (start us, length us, event | category | flops | bytes accessed | tf_op | source)
XLA Modules:
  0.0 69.8 jit_solution(10683535454768832615)
XLA Ops:
  0.6 68.1 %shard_map.118 = (bf16[8,128,128]{2,1,0:T(8,128)(2,1)S(1)}, bf16[16,64,128]{2,1,0:T(8,128)(2,1)S(1)}, bf16[16,32,128]{2,1,0:T(8,128)(2,1)S(1)}, f32[8,128]{1,0:T(8,128)S(1)}) custom-call(bf16[8,128,128]{2,1,0:T(8,128)(2,1)} %pair_hbm.1, bf16[8,128,128]{2,1,0:T(8,128)(2,1)} %cot_hbm.1, f32[2,128]{1,0:T(2,128)} %in_gain_hbm.1, ...), custom_call_target="tpu_custom_call" | custom-call | tf_op jit(solution)/shard_map/pallas_call | solution.py:453
  68.8 1.0 %shard_map.119 = (bf16[8,128,128]{2,1,0:T(8,128)(2,1)}, f32[2,128,512]{2,1,0:T(8,128)}, f32[2,128,128]{2,1,0:T(8,128)}, f32[2,128,128]{2,1,0:T(8,128)}, f32[2,128]{1,0:T(2,128)}, /*index=5*/f32[2,128]{1,0:T(2,128)}) custom-call(bf16[8,128,128]{2,1,0:T(8,128)(2,1)S(1)} %get-tuple-element.10.pair, bf16[16,64,128]{2,1,0:T(8,128)(2,1)S(1)} %get-tuple-element.11.early_in, ...), custom_call_target="tpu_custom_call" | custom-call | tf_op jit(solution)/shard_map/pallas_call | solution.py:506

commit v5 on v4

--- a/solution.py
+++ b/solution.py
@@ -23,8 +23,8 @@
 PART = ROWS * ROWS // CHUNKS
 
 TO_CH_0, TO_ROW_0, TO_CH_1, TO_ROW_1, GRAD_CH_1, GRAD_ROW_1, GRAD_CH_0, GRAD_ROW_0 = range(8)
-SUM_EARLY, ALL_EARLY, SUM_LATE, ALL_LATE, GAINS = range(8, 13)
-PHASES = 13
+SUM_EARLY, ALL_EARLY, SUM_LATE, ALL_LATE, GAINS, RIGHT_0, GRAD_LEFT_0 = range(8, 15)
+PHASES = 15
 
 
 def dot(first, second, dims):
@@ -70,7 +70,7 @@
     unit, inverse, normed, sig_l, val_l, sig_r, val_r, gate, gate_der, output, mix_unit, mix_inverse, mixed,
     grad_mixed, scaled, scaled_mean, grad_normed,
     go, gp, in_acc, mid_acc,
-    turn_a, turn_b, chan_l, chan_r,
+    turn_a, turn_b, chan_l, chan_r, chan_g,
     send2, recv2, send1, recv1,
     sum_early_send, sum_early_recv, all_early, sum_late_send, sum_late_recv, all_late, gains_all,
     load_sem, send_sem, recv_sem,
@@ -131,7 +131,7 @@
         block = ref[:, first : first + 2 * ROWS, :].astype(F32)
         return jnp.concatenate([block[:, i * ROWS : (i + 1) * ROWS].reshape(N, N) for i in range(2)], axis=1)
 
-    def project(l, p, state, ref):
+    def project(l, p, state, left_ref, right_ref, left_row, right_row):
         at = lanes(p)
         unit_p, inverse_p = norm_forward(state)
         normed_p = (unit_p * gains[2 * l]).astype(BF16)
@@ -139,17 +139,16 @@
         inverse[l, :, at] = inverse_p
         normed[l, :, at] = normed_p
         projected = nn(weight_t[l], normed_p)
-        row = 2 * ROWS * (p % PER)
         sig = sigmoid(projected[0:N])
         val = projected[N : 2 * N]
         sig_l[l, :, at] = sig
         val_l[l, :, at] = val
-        put_rows(ref, row, sig * val)
+        put_rows(left_ref, left_row, sig * val)
         sig = sigmoid(projected[2 * N : 3 * N])
         val = projected[3 * N : 4 * N]
         sig_r[l, :, at] = sig
         val_r[l, :, at] = val
-        put_rows(ref, PART + row, sig * val)
+        put_rows(right_ref, right_row, sig * val)
         gate[l, :, at] = projected[4 * N :]
 
     def after_project(l):
@@ -192,41 +191,97 @@
     def part_rows(d, h):
         return slice(d * ROWS * ROWS + h * PART, d * ROWS * ROWS + (h + 1) * PART)
 
+    def part_of(h):
+        return pl.ds(h * PART, PART)
+
+    def own_part(d, h):
+        first = h * PEERS * PART + d * PART
+        return slice(first, first + PART)
+
+    def channel_part(c, h):
+        return pl.ds(h * PEERS * PART + c, N // CHUNKS, stride=ROWS)
+
+    def half(h):
+        return slice(h * N // CHUNKS, (h + 1) * N // CHUNKS)
+
     def channel(c):
         return pl.ds(c, N, stride=ROWS)
 
-    def channel_forward(l, slot2, slot1, phase_in, phase_out):
+    def channel_forward_0():
+        wait_part(RIGHT_0, 0, recv2.at[0, 0])
+        for s in range(PEERS):
+            turn_b[s * 64 : s * 64 + 64, :] = recv2[0, 0, s].astype(F32)
+        for c in range(ROWS):
+            chan_r[0, c] = turn_b[channel(c), :].astype(BF16)
         for h in range(CHUNKS):
-            wait2_part(slot2, phase_in, h)
+            wait_part(TO_CH_0, h, recv2.at[0, 1, :, part_of(h)])
             for s in range(PEERS):
-                turn_a[part_rows(s, h), :] = recv2[slot2, h, s, :PART].astype(F32)
-                turn_b[part_rows(s, h), :] = recv2[slot2, h, s, PART:].astype(F32)
+                turn_a[own_part(s, h), :] = recv2[0, 1, s, h * PART : (h + 1) * PART].astype(F32)
+            for c in range(ROWS):
+                left = turn_a[channel_part(c, h), :].astype(BF16)
+                chan_l[0, c, half(h)] = left
+                turn_a[channel_part(c, h), :] = nt(left, chan_r[0, c])
+            for d in range(PEERS):
+                send1[0, h, d] = turn_a[own_part(d, h), :].astype(BF16)
+            send1_part(0, TO_ROW_0, h)
+
+    def channel_forward_1():
+        for h in range(CHUNKS):
+            wait2_part(1, TO_CH_1, h)
+            for s in range(PEERS):
+                turn_a[part_rows(s, h), :] = recv2[1, h, s, :PART].astype(F32)
+                turn_b[part_rows(s, h), :] = recv2[1, h, s, PART:].astype(F32)
         for c in range(ROWS):
             left = turn_a[channel(c), :].astype(BF16)
             right = turn_b[channel(c), :].astype(BF16)
-            chan_l[l, c] = left
-            chan_r[l, c] = right
-            turn_a[channel(c), :] = nt(left, right) if l == 0 else tn(left, right)
+            chan_l[1, c] = left
+            chan_r[1, c] = right
+            turn_a[channel(c), :] = tn(left, right)
         for h in range(CHUNKS):
             for d in range(PEERS):
-                send1[slot1, h, d] = turn_a[part_rows(d, h), :].astype(BF16)
-            send1_part(slot1, phase_out, h)
-
-    def channel_backward(l, slot1, slot2, phase_in, phase_out):
+                send1[1, h, d] = turn_a[part_rows(d, h), :].astype(BF16)
+            send1_part(1, TO_ROW_1, h)
+
+    def channel_backward_1():
         for h in range(CHUNKS):
-            wait1_part(slot1, phase_in, h)
+            wait1_part(2, GRAD_CH_1, h)
             for s in range(PEERS):
-                turn_a[part_rows(s, h), :] = recv1[slot1, h, s].astype(F32)
+                turn_a[part_rows(s, h), :] = recv1[2, h, s].astype(F32)
         for c in range(ROWS):
             grad = turn_a[channel(c), :].astype(BF16)
-            left, right = chan_l[l, c], chan_r[l, c]
-            turn_a[channel(c), :] = nn(grad, right) if l == 0 else nt(right, grad)
-            turn_b[channel(c), :] = tn(grad, left) if l == 0 else nn(left, grad)
+            turn_a[channel(c), :] = nt(chan_r[1, c], grad)
+            turn_b[channel(c), :] = nn(chan_l[1, c], grad)
         for h in range(CHUNKS):
             for d in range(PEERS):
-                send2[slot2, h, d, :PART] = turn_a[part_rows(d, h), :].astype(BF16)
-                send2[slot2, h, d, PART:] = turn_b[part_rows(d, h), :].astype(BF16)
-            send2_part(slot2, phase_out, h)
+                send2[2, h, d, :PART] = turn_a[part_rows(d, h), :].astype(BF16)
+                send2[2, h, d, PART:] = turn_b[part_rows(d, h), :].astype(BF16)
+            send2_part(2, GRAD_ROW_1, h)
+
+    def channel_backward_0():
+        left_rows = pl.ds(0, PART)
+        for h in range(CHUNKS):
+            wait1_part(3, GRAD_CH_0, h)
+            for s in range(PEERS):
+                turn_a[own_part(s, h), :] = recv1[3, h, s].astype(F32)
+            for c in range(ROWS):
+                grad = turn_a[channel_part(c, h), :].astype(BF16)
+                chan_g[c, half(h)] = grad
+                turn_b[channel_part(c, h), :] = nn(grad, chan_r[0, c])
+            for d in range(PEERS):
+                send2[3, h, d, :PART] = turn_b[own_part(d, h), :].astype(BF16)
+            if h == 0:
+                send_part(GRAD_LEFT_0, 0, lambda d: send2.at[3, 0, d, left_rows], recv2.at[3, 0, me, left_rows])
+        for c in range(ROWS):
+            turn_a[channel(c), :] = tn(chan_g[c], chan_l[0, c])
+        for h in range(CHUNKS):
+            for d in range(PEERS):
+                send2[3, h, d, PART:] = turn_a[part_rows(d, h), :].astype(BF16)
+            if h == 0:
+                right_rows = pl.ds(PART, PART)
+                send_part(GRAD_ROW_0, 0, lambda d: send2.at[3, 0, d, right_rows], recv2.at[3, 0, me, right_rows])
+                recv2[3, 0, me] = send2[3, 0, me]
+            else:
+                send2_part(3, GRAD_ROW_0, h)
 
     def fold(values):
         return values[:, :N] + values[:, N:]
@@ -270,12 +325,15 @@
         weight_t[l, 4 * N :, :] = gate_weight[l].astype(F32).T.astype(BF16)
 
     set_weights(0)
+    for p in range(STEPS):
+        project(0, p, state0[:, lanes(p)], send2.at[0, 1], send2.at[0, 0], 2 * ROWS * p, 2 * ROWS * p)
+    pl.semaphore_wait(barrier, PEERS - 1)
+    send_part(RIGHT_0, 0, lambda d: send2.at[0, 0, d], recv2.at[0, 0, me])
     for h in range(CHUNKS):
-        for p in steps(h):
-            project(0, p, state0[:, lanes(p)], send2.at[0, h])
-        if h == 0:
-            pl.semaphore_wait(barrier, PEERS - 1)
-        send2_part(0, TO_CH_0, h)
+        rows = part_of(h)
+        send_part(TO_CH_0, h, lambda d: send2.at[0, 1, d, rows], recv2.at[0, 1, me, rows])
+    for i in range(2):
+        recv2[0, i, me] = send2[0, i, me]
 
     for load in loads[4:]:
         load.wait()
@@ -288,7 +346,7 @@
 
     after_project(0)
 
-    channel_forward(0, 0, 0, TO_CH_0, TO_ROW_0)
+    channel_forward_0()
 
     for h in range(CHUNKS):
         wait1_part(0, TO_ROW_0, h)
@@ -302,12 +360,13 @@
             output_p = nn(out_t[0], mixed_p)
             output[:, at] = output_p
             state = (state0[:, at] + gate[0, :, at] * output_p).astype(BF16).astype(F32)
-            project(1, p, state, send2.at[1, h])
+            row = 2 * ROWS * (p % PER)
+            project(1, p, state, send2.at[1, h], send2.at[1, h], row, PART + row)
         send2_part(1, TO_CH_1, h)
 
     after_project(1)
 
-    channel_forward(1, 1, 1, TO_CH_1, TO_ROW_1)
+    channel_forward_1()
 
     for h in range(CHUNKS):
         wait1_part(1, TO_ROW_1, h)
@@ -329,7 +388,7 @@
         gp[1, 4 * N :, at] = (gate_der[1, :, at] * nn(out_t[1], mixed_p)).astype(BF16)
         mid_acc[1] += fold(grad_mixed[:, at] * mix_unit_p)
 
-    channel_backward(1, 2, 2, GRAD_CH_1, GRAD_ROW_1)
+    channel_backward_1()
 
     for h in range(CHUNKS):
         wait2_part(2, GRAD_ROW_1, h)
@@ -361,18 +420,10 @@
     put_early(10, nt(mixed[1], go[1]))
     put_early(12, nt(normed[0], gp[0, 4 * N :, :]))
     put_early(14, nt(mixed[0], go[0]))
-    for h in range(CHUNKS):
-        wait_sent(GRAD_CH_0, h, send1.at[3, h])
+
+    channel_backward_0()
     send_part(SUM_EARLY, 0, lambda d: sum_early_send.at[d], sum_early_recv.at[me])
     sum_early_recv[me] = sum_early_send[me]
-
-    channel_backward(0, 3, 3, GRAD_CH_0, GRAD_ROW_0)
-
-    wait_part(SUM_EARLY, 0, sum_early_recv)
-    all_early[me] = jnp.sum(sum_early_recv[...].astype(F32), axis=0).astype(BF16)
-    for h in range(CHUNKS):
-        wait_sent(GRAD_ROW_0, h, send2.at[3, h])
-    send_part(ALL_EARLY, 0, lambda d: all_early.at[me], all_early.at[me])
 
     def last_rows(p):
         gradient = back_tail(0, p, grad1[:, lanes(p)])
@@ -380,7 +431,11 @@
             pair_grad[2 * p + i] = gradient[:, i * N : (i + 1) * N].T.astype(BF16)
 
     for h in range(CHUNKS):
-        wait2_part(3, GRAD_ROW_0, h)
+        if h == 0:
+            wait_part(GRAD_LEFT_0, 0, recv2.at[3, 0, :, pl.ds(0, PART)])
+            wait_part(GRAD_ROW_0, 0, recv2.at[3, 0, :, pl.ds(PART, PART)])
+        else:
+            wait2_part(3, GRAD_ROW_0, h)
         for p in steps(h):
             back_pieces(0, p, recv2.at[3, h])
         if h < CHUNKS - 1:
@@ -394,6 +449,10 @@
     send_part(SUM_LATE, 0, lambda d: sum_late_send.at[d], sum_late_recv.at[me])
     sum_late_recv[me] = sum_late_send[me]
 
+    wait_part(SUM_EARLY, 0, sum_early_recv)
+    all_early[me] = jnp.sum(sum_early_recv[...].astype(F32), axis=0).astype(BF16)
+    send_part(ALL_EARLY, 0, lambda d: all_early.at[me], all_early.at[me])
+
     for p in steps(CHUNKS - 1):
         last_rows(p)
 
@@ -408,9 +467,17 @@
     wait_part(ALL_EARLY, 0, all_early)
     early_out[...] = all_early[...]
     for h in range(CHUNKS):
-        for slot, two, one in ((0, TO_CH_0, TO_ROW_0), (1, TO_CH_1, TO_ROW_1), (2, GRAD_ROW_1, GRAD_CH_1)):
+        wait_sent(TO_CH_0, h, send2.at[0, 1, :, part_of(h)])
+        wait_sent(TO_ROW_0, h, send1.at[0, h])
+        for slot, two, one in ((1, TO_CH_1, TO_ROW_1), (2, GRAD_ROW_1, GRAD_CH_1)):
             wait_sent(two, h, send2.at[slot, h])
             wait_sent(one, h, send1.at[slot, h])
+    wait_sent(RIGHT_0, 0, send2.at[0, 0])
+    wait_sent(GRAD_LEFT_0, 0, send2.at[3, 0, :, pl.ds(0, PART)])
+    wait_sent(GRAD_ROW_0, 0, send2.at[3, 0, :, pl.ds(PART, PART)])
+    wait_sent(GRAD_ROW_0, 1, send2.at[3, 1])
+    for h in range(CHUNKS):
+        wait_sent(GRAD_CH_0, h, send1.at[3, h])
     wait_sent(SUM_EARLY, 0, sum_early_send)
     wait_sent(ALL_EARLY, 0, all_early)
     wait_sent(SUM_LATE, 0, sum_late_send)
@@ -484,6 +551,7 @@
             pltpu.VMEM((CELLS, N), F32),
             pltpu.VMEM((2, ROWS, N, N), BF16),
             pltpu.VMEM((2, ROWS, N, N), BF16),
+            pltpu.VMEM((ROWS, N, N), BF16),
             pltpu.VMEM((4, CHUNKS, PEERS, 2 * PART, N), BF16),
             pltpu.VMEM((4, CHUNKS, PEERS, 2 * PART, N), BF16),
             pltpu.VMEM((4, CHUNKS, PEERS, PART, N), BF16),

time: 70 us -> 69.2 us (0.989)
  Pallas kernels: 69.2 us -> 68.4 us
    pallas_call x1, Pallas kernels: 68.1 us -> 67.4 us  [on_device(): pl.pallas_call(kernel, out_shape=(pltpu.VMEM((ROWS, N, N), BF16), pltpu.V...]
where the time goes in v5:
time: 69.2 us; the launch traced here: 69.1 us
  Pallas kernels  68.4 us (99%)
    pallas_call x1, Pallas kernels, on_device(): pl.pallas_call(kernel, out_shape=(pltpu.VMEM((ROWS, N, N), BF16), pltpu.V...  67.4 us

profile of v5, /device:TPU:1, one launch (start us, length us, event | category | flops | bytes accessed | tf_op | source)
XLA Modules:
  0.0 69.1 jit_solution(14597823244900658828)
XLA Ops:
  0.6 67.4 %shard_map.118 = (bf16[8,128,128]{2,1,0:T(8,128)(2,1)S(1)}, bf16[16,64,128]{2,1,0:T(8,128)(2,1)S(1)}, bf16[16,32,128]{2,1,0:T(8,128)(2,1)S(1)}, f32[8,128]{1,0:T(8,128)S(1)}) custom-call(bf16[8,128,128]{2,1,0:T(8,128)(2,1)} %pair_hbm.1, bf16[8,128,128]{2,1,0:T(8,128)(2,1)} %cot_hbm.1, f32[2,128]{1,0:T(2,128)} %in_gain_hbm.1, ...), custom_call_target="tpu_custom_call" | custom-call | tf_op jit(solution)/shard_map/pallas_call | solution.py:520
  68.0 1.0 %shard_map.119 = (bf16[8,128,128]{2,1,0:T(8,128)(2,1)}, f32[2,128,512]{2,1,0:T(8,128)}, f32[2,128,128]{2,1,0:T(8,128)}, f32[2,128,128]{2,1,0:T(8,128)}, f32[2,128]{1,0:T(2,128)}, /*index=5*/f32[2,128]{1,0:T(2,128)}) custom-call(bf16[8,128,128]{2,1,0:T(8,128)(2,1)S(1)} %get-tuple-element.10.pair, bf16[16,64,128]{2,1,0:T(8,128)(2,1)S(1)} %get-tuple-element.11.early_in, ...), custom_call_target="tpu_custom_call" | custom-call | tf_op jit(solution)/shard_map/pallas_call | solution.py:574

commit v6 on v5

--- a/solution.py
+++ b/solution.py
@@ -23,8 +23,8 @@
 PART = ROWS * ROWS // CHUNKS
 
 TO_CH_0, TO_ROW_0, TO_CH_1, TO_ROW_1, GRAD_CH_1, GRAD_ROW_1, GRAD_CH_0, GRAD_ROW_0 = range(8)
-SUM_EARLY, ALL_EARLY, SUM_LATE, ALL_LATE, GAINS, RIGHT_0, GRAD_LEFT_0 = range(8, 15)
-PHASES = 15
+SUM_EARLY, ALL_EARLY, SUM_LATE, ALL_LATE, GAINS, RIGHT_0, GRAD_LEFT_0, PRE_EARLY, SHARE_EARLY = range(8, 17)
+PHASES = 17
 
 
 def dot(first, second, dims):
@@ -72,7 +72,7 @@
     go, gp, in_acc, mid_acc,
     turn_a, turn_b, chan_l, chan_r, chan_g,
     send2, recv2, send1, recv1,
-    sum_early_send, sum_early_recv, all_early, sum_late_send, sum_late_recv, all_late, gains_all,
+    sum_early_send, pre_early, sum_early_mid, sum_early_recv, all_early, sum_late_send, sum_late_recv, all_late, gains_all,
     load_sem, send_sem, recv_sem,
 ):
     me = lax.axis_index("pair")
@@ -87,6 +87,8 @@
     barrier = pltpu.get_barrier_semaphore()
 
     peers = [peer(o) for o in (4, 12, 5, 13, 2, 10, 6, 14, 3, 11, 7, 15, 8, 9, 1)]
+    same_core = [peer(o) for o in (4, 12, 2, 10, 6, 14, 8)]
+    chip = me // 2
     for target in peers:
         pl.semaphore_signal(barrier, inc=1, device_id={"pair": target}, device_id_type=MESH)
 
@@ -100,9 +102,9 @@
     for load in loads:
         load.start()
 
-    def send_part(phase, h, src_of, dst):
+    def send_part(phase, h, src_of, dst, targets=None):
         sem = phase * CHUNKS + h
-        for target in peers:
+        for target in targets or peers:
             pltpu.make_async_remote_copy(
                 src_ref=src_of(target), dst_ref=dst,
                 send_sem=send_sem.at[sem], recv_sem=recv_sem.at[sem],
@@ -112,6 +114,9 @@
     def wait_part(phase, h, slots):
         fifteen = slots.at[pl.ds(0, PEERS - 1)]
         pltpu.make_async_copy(fifteen, fifteen, recv_sem.at[phase * CHUNKS + h]).wait()
+
+    def wait_bytes(phase, sems, some):
+        pltpu.make_async_copy(some, some, sems.at[phase * CHUNKS]).wait()
 
     def wait_sent(phase, h, slots):
         fifteen = slots.at[pl.ds(0, PEERS - 1)]
@@ -413,17 +418,20 @@
 
     def put_early(first, values):
         for i in range(N // 64):
-            sum_early_send[first + i] = values[64 * i : 64 * i + 64, :].astype(BF16)
+            sum_early_send[i, first // 2] = values[64 * i : 64 * i + 64, :].astype(BF16)
 
     for f in range(5):
         put_early(2 * f, nt(normed[1], gp[1, f * N : (f + 1) * N, :]))
     put_early(10, nt(mixed[1], go[1]))
     put_early(12, nt(normed[0], gp[0, 4 * N :, :]))
     put_early(14, nt(mixed[0], go[0]))
+    send_part(PRE_EARLY, 0, lambda d: sum_early_send.at[1 - my_core], pre_early, [peer(1)])
 
     channel_backward_0()
-    send_part(SUM_EARLY, 0, lambda d: sum_early_send.at[d], sum_early_recv.at[me])
-    sum_early_recv[me] = sum_early_send[me]
+    wait_bytes(PRE_EARLY, recv_sem, pre_early)
+    sum_early_mid[...] = (sum_early_send[my_core].astype(F32) + pre_early[...].astype(F32)).astype(BF16)
+    send_part(SUM_EARLY, 0, lambda d: sum_early_mid.at[d // 2], sum_early_recv.at[chip], same_core)
+    sum_early_recv[chip] = sum_early_mid[chip]
 
     def last_rows(p):
         gradient = back_tail(0, p, grad1[:, lanes(p)])
@@ -449,9 +457,10 @@
     send_part(SUM_LATE, 0, lambda d: sum_late_send.at[d], sum_late_recv.at[me])
     sum_late_recv[me] = sum_late_send[me]
 
-    wait_part(SUM_EARLY, 0, sum_early_recv)
-    all_early[me] = jnp.sum(sum_early_recv[...].astype(F32), axis=0).astype(BF16)
-    send_part(ALL_EARLY, 0, lambda d: all_early.at[me], all_early.at[me])
+    wait_bytes(SUM_EARLY, recv_sem, sum_early_recv.at[pl.ds(0, 7)])
+    all_early[my_core, chip] = jnp.sum(sum_early_recv[...].astype(F32), axis=0).astype(BF16)
+    mine = all_early.at[my_core, chip]
+    send_part(ALL_EARLY, 0, lambda d: mine, mine, same_core)
 
     for p in steps(CHUNKS - 1):
         last_rows(p)
@@ -464,8 +473,8 @@
     all_late[me] = jnp.sum(sum_late_recv[...].astype(F32), axis=0).astype(BF16)
     send_part(ALL_LATE, 0, lambda d: all_late.at[me], all_late.at[me])
 
-    wait_part(ALL_EARLY, 0, all_early)
-    early_out[...] = all_early[...]
+    wait_bytes(ALL_EARLY, recv_sem, all_early.at[0, pl.ds(0, 7)])
+    send_part(SHARE_EARLY, 0, lambda d: all_early.at[my_core], all_early.at[my_core], [peer(1)])
     for h in range(CHUNKS):
         wait_sent(TO_CH_0, h, send2.at[0, 1, :, part_of(h)])
         wait_sent(TO_ROW_0, h, send1.at[0, h])
@@ -478,10 +487,15 @@
     wait_sent(GRAD_ROW_0, 1, send2.at[3, 1])
     for h in range(CHUNKS):
         wait_sent(GRAD_CH_0, h, send1.at[3, h])
-    wait_sent(SUM_EARLY, 0, sum_early_send)
-    wait_sent(ALL_EARLY, 0, all_early)
+    wait_bytes(PRE_EARLY, send_sem, pre_early)
+    wait_bytes(SUM_EARLY, send_sem, sum_early_mid.at[pl.ds(0, 7)])
+    wait_bytes(ALL_EARLY, send_sem, all_early.at[0, pl.ds(0, 7)])
     wait_sent(SUM_LATE, 0, sum_late_send)
     wait_sent(GAINS, 0, gains_all)
+
+    wait_bytes(SHARE_EARLY, recv_sem, all_early.at[0])
+    early_out[...] = all_early[...]
+    wait_bytes(SHARE_EARLY, send_sem, all_early.at[0])
 
     wait_part(GAINS, 0, gains_all)
     gains_out[...] = jnp.sum(gains_all[...], axis=0)
@@ -499,7 +513,7 @@
     pair_grad[...] = pair[...]
 
     def early(first):
-        return early_in[first : first + 2].astype(F32).reshape(N, N) * scale
+        return early_in[:, first // 2].astype(F32).reshape(N, N) * scale
 
     for f in range(4):
         proj_grad[0, :, f * N : (f + 1) * N] = late_in[4 * f : 4 * f + 4].astype(F32).reshape(N, N) * scale
@@ -521,7 +535,7 @@
         kernel,
         out_shape=(
             pltpu.VMEM((ROWS, N, N), BF16),
-            pltpu.VMEM((PEERS, 64, N), BF16),
+            pltpu.VMEM((2, PEERS // 2, 64, N), BF16),
             pltpu.VMEM((PEERS, 32, N), BF16),
             pltpu.VMEM((8, N), F32),
         ),
@@ -556,9 +570,11 @@
             pltpu.VMEM((4, CHUNKS, PEERS, 2 * PART, N), BF16),
             pltpu.VMEM((4, CHUNKS, PEERS, PART, N), BF16),
             pltpu.VMEM((4, CHUNKS, PEERS, PART, N), BF16),
-            pltpu.VMEM((PEERS, 64, N), BF16),
-            pltpu.VMEM((PEERS, 64, N), BF16),
-            pltpu.VMEM((PEERS, 64, N), BF16),
+            pltpu.VMEM((2, PEERS // 2, 64, N), BF16),
+            pltpu.VMEM((PEERS // 2, 64, N), BF16),
+            pltpu.VMEM((PEERS // 2, 64, N), BF16),
+            pltpu.VMEM((PEERS // 2, 64, N), BF16),
+            pltpu.VMEM((2, PEERS // 2, 64, N), BF16),
             pltpu.VMEM((PEERS, 32, N), BF16),
             pltpu.VMEM((PEERS, 32, N), BF16),
             pltpu.VMEM((PEERS, 32, N), BF16),

time: 69.2 us -> 68.5 us (0.990)
  Pallas kernels: 68.4 us -> 67.7 us
    pallas_call x1, Pallas kernels: 67.4 us -> 66.7 us  [on_device(): pl.pallas_call(kernel, out_shape=(pltpu.VMEM((ROWS, N, N), BF16), pltpu.V...]
where the time goes in v6:
time: 68.5 us; the launch traced here: 68.4 us
  Pallas kernels  67.7 us (99%)
    pallas_call x1, Pallas kernels, on_device(): pl.pallas_call(kernel, out_shape=(pltpu.VMEM((ROWS, N, N), BF16), pltpu.V...  66.7 us

profile of v6, /device:TPU:1, one launch (start us, length us, event | category | flops | bytes accessed | tf_op | source)
XLA Modules:
  0.0 68.4 jit_solution(14931876500235521441)
XLA Ops:
  0.6 66.7 %shard_map.118 = (bf16[8,128,128]{2,1,0:T(8,128)(2,1)S(1)}, bf16[2,8,64,128]{3,2,1,0:T(8,128)(2,1)S(1)}, bf16[16,32,128]{2,1,0:T(8,128)(2,1)S(1)}, f32[8,128]{1,0:T(8,128)S(1)}) custom-call(bf16[8,128,128]{2,1,0:T(8,128)(2,1)} %pair_hbm.1, bf16[8,128,128]{2,1,0:T(8,128)(2,1)} %cot_hbm.1, f32[2,128]{1,0:T(2,128)} %in_gain_hbm.1, ...), custom_call_target="tpu_custom_call" | custom-call | tf_op jit(solution)/shard_map/pallas_call | solution.py:534
  67.3 1.0 %shard_map.119 = (bf16[8,128,128]{2,1,0:T(8,128)(2,1)}, f32[2,128,512]{2,1,0:T(8,128)}, f32[2,128,128]{2,1,0:T(8,128)}, f32[2,128,128]{2,1,0:T(8,128)}, f32[2,128]{1,0:T(2,128)}, /*index=5*/f32[2,128]{1,0:T(2,128)}) custom-call(bf16[8,128,128]{2,1,0:T(8,128)(2,1)S(1)} %get-tuple-element.10.pair, bf16[2,8,64,128]{3,2,1,0:T(8,128)(2,1)S(1)} %get-tuple-element.11.early_in, ...), custom_call_target="tpu_custom_call" | custom-call | tf_op jit(solution)/shard_map/pallas_call | solution.py:590

commit v7 on v6

--- a/solution.py
+++ b/solution.py
@@ -561,8 +561,8 @@
             pltpu.VMEM((2, 5 * N, CELLS), BF16),
             pltpu.VMEM((2, N, N), F32),
             pltpu.VMEM((2, N, N), F32),
-            pltpu.VMEM((CELLS, N), F32),
-            pltpu.VMEM((CELLS, N), F32),
+            pltpu.VMEM((CELLS + ROWS, N), F32),
+            pltpu.VMEM((CELLS + ROWS, N), F32),
             pltpu.VMEM((2, ROWS, N, N), BF16),
             pltpu.VMEM((2, ROWS, N, N), BF16),
             pltpu.VMEM((ROWS, N, N), BF16),

time: 68.5 us -> 68.5 us (level)
  no operation moved by 1% of the time
where the time goes in v7:
time: 68.5 us; the launch traced here: 68.4 us
  Pallas kernels  67.8 us (99%)
    pallas_call x1, Pallas kernels, on_device(): pl.pallas_call(kernel, out_shape=(pltpu.VMEM((ROWS, N, N), BF16), pltpu.V...  66.7 us

profile of v7, /device:TPU:1, one launch (start us, length us, event | category | flops | bytes accessed | tf_op | source)
XLA Modules:
  0.0 68.4 jit_solution(12127398126811419146)
XLA Ops:
  0.6 66.7 %shard_map.118 = (bf16[8,128,128]{2,1,0:T(8,128)(2,1)S(1)}, bf16[2,8,64,128]{3,2,1,0:T(8,128)(2,1)S(1)}, bf16[16,32,128]{2,1,0:T(8,128)(2,1)S(1)}, f32[8,128]{1,0:T(8,128)S(1)}) custom-call(bf16[8,128,128]{2,1,0:T(8,128)(2,1)} %pair_hbm.1, bf16[8,128,128]{2,1,0:T(8,128)(2,1)} %cot_hbm.1, f32[2,128]{1,0:T(2,128)} %in_gain_hbm.1, ...), custom_call_target="tpu_custom_call" | custom-call | tf_op jit(solution)/shard_map/pallas_call | solution.py:534
  67.4 1.0 %shard_map.119 = (bf16[8,128,128]{2,1,0:T(8,128)(2,1)}, f32[2,128,512]{2,1,0:T(8,128)}, f32[2,128,128]{2,1,0:T(8,128)}, f32[2,128,128]{2,1,0:T(8,128)}, f32[2,128]{1,0:T(2,128)}, /*index=5*/f32[2,128]{1,0:T(2,128)}) custom-call(bf16[8,128,128]{2,1,0:T(8,128)(2,1)S(1)} %get-tuple-element.10.pair, bf16[2,8,64,128]{3,2,1,0:T(8,128)(2,1)S(1)} %get-tuple-element.11.early_in, ...), custom_call_target="tpu_custom_call" | custom-call | tf_op jit(solution)/shard_map/pallas_call | solution.py:590

commit v8 on v7

--- a/solution.py
+++ b/solution.py
@@ -70,7 +70,7 @@
     unit, inverse, normed, sig_l, val_l, sig_r, val_r, gate, gate_der, output, mix_unit, mix_inverse, mixed,
     grad_mixed, scaled, scaled_mean, grad_normed,
     go, gp, in_acc, mid_acc,
-    turn_a, turn_b, chan_l, chan_r, chan_g,
+    turn_a, turn_b, chan_l, chan_r, chan_g, late_sum,
     send2, recv2, send1, recv1,
     sum_early_send, pre_early, sum_early_mid, sum_early_recv, all_early, sum_late_send, sum_late_recv, all_late, gains_all,
     load_sem, send_sem, recv_sem,
@@ -427,11 +427,12 @@
     put_early(14, nt(mixed[0], go[0]))
     send_part(PRE_EARLY, 0, lambda d: sum_early_send.at[1 - my_core], pre_early, [peer(1)])
 
-    channel_backward_0()
     wait_bytes(PRE_EARLY, recv_sem, pre_early)
     sum_early_mid[...] = (sum_early_send[my_core].astype(F32) + pre_early[...].astype(F32)).astype(BF16)
     send_part(SUM_EARLY, 0, lambda d: sum_early_mid.at[d // 2], sum_early_recv.at[chip], same_core)
     sum_early_recv[chip] = sum_early_mid[chip]
+
+    channel_backward_0()
 
     def last_rows(p):
         gradient = back_tail(0, p, grad1[:, lanes(p)])
@@ -449,9 +450,11 @@
         if h < CHUNKS - 1:
             for p in steps(h):
                 last_rows(p)
+            for f in range(4):
+                late_sum[f] = nt(normed[0, :, : CELLS // 2], gp[0, f * N : (f + 1) * N, : CELLS // 2])
 
     for f in range(4):
-        values = nt(normed[0], gp[0, f * N : (f + 1) * N, :])
+        values = late_sum[f] + nt(normed[0, :, CELLS // 2 :], gp[0, f * N : (f + 1) * N, CELLS // 2 :])
         for i in range(4):
             sum_late_send[4 * f + i] = values[32 * i : 32 * i + 32, :].astype(BF16)
     send_part(SUM_LATE, 0, lambda d: sum_late_send.at[d], sum_late_recv.at[me])
@@ -566,6 +569,7 @@
             pltpu.VMEM((2, ROWS, N, N), BF16),
             pltpu.VMEM((2, ROWS, N, N), BF16),
             pltpu.VMEM((ROWS, N, N), BF16),
+            pltpu.VMEM((4, N, N), F32),
             pltpu.VMEM((4, CHUNKS, PEERS, 2 * PART, N), BF16),
             pltpu.VMEM((4, CHUNKS, PEERS, 2 * PART, N), BF16),
             pltpu.VMEM((4, CHUNKS, PEERS, PART, N), BF16),

time: 68.5 us -> 68.1 us (level)
  no operation moved by 1% of the time
where the time goes in v8:
time: 68.1 us; the launch traced here: 67.9 us
  Pallas kernels  67.3 us (99%)
    pallas_call x1, Pallas kernels, on_device(): pl.pallas_call(kernel, out_shape=(pltpu.VMEM((ROWS, N, N), BF16), pltpu.V...  66.2 us

profile of v8, /device:TPU:1, one launch (start us, length us, event | category | flops | bytes accessed | tf_op | source)
XLA Modules:
  0.0 67.9 jit_solution(5887610660152767203)
XLA Ops:
  0.6 66.2 %shard_map.118 = (bf16[8,128,128]{2,1,0:T(8,128)(2,1)S(1)}, bf16[2,8,64,128]{3,2,1,0:T(8,128)(2,1)S(1)}, bf16[16,32,128]{2,1,0:T(8,128)(2,1)S(1)}, f32[8,128]{1,0:T(8,128)S(1)}) custom-call(bf16[8,128,128]{2,1,0:T(8,128)(2,1)} %pair_hbm.1, bf16[8,128,128]{2,1,0:T(8,128)(2,1)} %cot_hbm.1, f32[2,128]{1,0:T(2,128)} %in_gain_hbm.1, ...), custom_call_target="tpu_custom_call" | custom-call | tf_op jit(solution)/shard_map/pallas_call | solution.py:537
  66.9 1.0 %shard_map.119 = (bf16[8,128,128]{2,1,0:T(8,128)(2,1)}, f32[2,128,512]{2,1,0:T(8,128)}, f32[2,128,128]{2,1,0:T(8,128)}, f32[2,128,128]{2,1,0:T(8,128)}, f32[2,128]{1,0:T(2,128)}, /*index=5*/f32[2,128]{1,0:T(2,128)}) custom-call(bf16[8,128,128]{2,1,0:T(8,128)(2,1)S(1)} %get-tuple-element.10.pair, bf16[2,8,64,128]{3,2,1,0:T(8,128)(2,1)S(1)} %get-tuple-element.11.early_in, ...), custom_call_target="tpu_custom_call" | custom-call | tf_op jit(solution)/shard_map/pallas_call | solution.py:594
